TPU v7x, 512 devices: a whole 4x8x8 slice. The times are simulated.
512 devices in a mesh: row: 16 (over x_hi, y), col: 16 (over z, core), layer: 2 (over x_lo).
Axes of the slice: x: 4 (x_hi: 2, x_lo: 2; x = x_hi * 2 + x_lo), y: 8, z: 8, core: 2. Of those that a mesh axis runs over, the one named last changes fastest.
Arguments:
- a_blocks: float32 [256, 8, 128, 128], P(('row', 'col'), 'layer'), may hold values from -0.1875 to 0.1875
- p_blocks: float32 [256, 8, 128, 128], P(('row', 'col'), 'layer'), may hold values from -6 to 6
- out_columns: int32 [256, 64], P('row', 'col'), may hold values from 0 to 15
- pair_codes: int32 [256, 64, 14], P('row', 'col', 'layer'), may hold values from 0 to 16, as said below
Outputs:
- c_blocks: float32 [256, 64, 128, 128], P(('row', 'layer'), 'col')
Inputs may be any that keep to these rules, and one draw needn't show every extreme that they name: `pair_codes`: within each block (r, s) and inner range, the first entries are live and pairwise distinct, all later ones equal 16; at least one is live, and product slot 0 of every block row has all 7 live.
All inputs are finite; a program needn't handle non-finite values.
Results may differ from a plain program's by a relative error of at most 0.0003.
Values sent between devices are 32-bit elements; how exact they have to be, the bound alone decides.
A program may use at most 64 MiB of HBM per device.

v0:
```python
import jax
import jax.numpy as jnp
from jax import lax
from jax.sharding import PartitionSpec as P


def shards(a_blocks, p_blocks, out_columns, pair_codes):
    slots_a = a_blocks.shape[1]
    slots_p = p_blocks.shape[1]
    pair_total = slots_a * slots_p
    p_panel = lax.all_gather(p_blocks, "row", axis=0, tiled=True)

    def row_work(inputs):
        a_row, out_cols, pair_list = inputs
        is_live = pair_list < pair_total
        a_pick = jnp.minimum(pair_list // slots_p, slots_a - 1)
        p_pick = pair_list % slots_p
        a_sel = a_row[a_pick] * is_live[:, :, None, None].astype(jnp.float32)
        p_sel = p_panel[out_cols[:, None], p_pick]
        return jnp.einsum("omij,omjk->oik", a_sel, p_sel, precision=lax.Precision.HIGHEST)

    a_panel = lax.all_gather(a_blocks, "col", axis=0, tiled=True)
    partial_value = lax.map(row_work, (a_panel, out_columns, pair_codes))
    return lax.psum_scatter(partial_value, "layer", scatter_dimension=0, tiled=True)


def solution(mesh):
    return jax.shard_map(
        shards,
        mesh=mesh,
        in_specs=(
            P(("row", "col"), "layer", None, None),
            P(("row", "col"), "layer", None, None),
            P("row", "col"),
            P("row", "col", "layer"),
        ),
        out_specs=P(("row", "layer"), "col", None, None),
        check_vma=False,
    )
```

profile of v0, /device:TPU:6, one launch (start us, length us, event | category | flops | bytes accessed | tf_op | source)
XLA Modules:
  0.0 394.7 jit_solution(14123713427985720065)
XLA Ops:
  9.6 50.1 %all-gather.3.cloned.1.call-done = f32[16,4,128,128]{3,2,1,0:T(8,128)} async-done(((f32[1,4,128,128]{3,2,1,0:T(8,128)}), f32[16,4,128,128]{3,2,1,0:T(8,128)}) %all-gather.3.cloned.1.call-update) | async-done | bytes 4194320 | tf_op jit(solution)/shard_map/all_gather | solution.py:22
  59.8 105.0 %all-gather.5.cloned.1.call-done = f32[16,4,128,128]{3,2,1,0:T(8,128)} async-done(((f32[1,4,128,128]{3,2,1,0:T(8,128)}), f32[16,4,128,128]{3,2,1,0:T(8,128)}) %all-gather.5.cloned.1.call-update) | async-done | bytes 4194320 | tf_op jit(solution)/shard_map/all_gather | solution.py:11
  164.8 163.3 %while.12 = (s32[]{:T(128)}, f32[16,4,128,128]{3,2,1,0:T(8,128)}, f32[16,4,128,128]{3,2,1,0:T(8,128)}, s32[16,4,7]{2,1,0:T(4,128)S(1)}, s32[16,4]{1,0:T(8,128)S(1)}, /*index=5*/f32[16,4,128,128]{3,2,1,0:T(8,128)}, s32[]{:T(128)}) while((s32[]{:T(128)}, f32[16,4,128,128]{3,2,1,0:T(8,128)}, f32[16,4,128,128]{3,2,1,0:T(8,128)}, ...), condition=%wide.region_1.2_spmd, body=%wide.region_0.1_spmd.sunk | while | flops 705103744 | bytes 11802797 | solution.py:23
  165.0 1.0 dynamic-slice_bitcast_fusion.2
  166.7 4.1 %gather_fusion = f32[28,128,128]{2,1,0:T(8,128)} fusion(f32[16,4,128,128]{3,2,1,0:T(8,128)} %get-tuple-element.172, s32[28]{0:T(128)S(1)} %reshape.212), kind=kCustom, calls=%fused_computation.1.clone.1 | custom fusion | bytes 3670240 | tf_op jit(solution)/shard_map/while/body/eval_jaxpr/gather | solution.py:19
  170.8 4.2 %fusion.22 = f32[16,4,128,128]{3,2,1,0:T(8,128)} fusion(f32[16,4,128,128]{3,2,1,0:T(8,128)} %get-tuple-element.161, s32[]{:T(128)} %get-tuple-element.160, f32[4,7,128,128]{3,2,1,0:T(8,128)} %bitcast.62, f32[4,7,128,128]{3,2,1,0:T(8,128)S(1)} %bitcast.61, f32[4,7]{1,0:T(4,128)S(1)} %convert_bitcast_fusion.2), kind=kOutput, calls=%fused_computation.5.clone.1 | convolution fusion | flops 705101824 | bytes 3932784 | tf_op jit(solution)/shard_map/while/body/eval_jaxpr/omij,omjk->oik/dot_general | solution.py:20
  175.2 1.0 dynamic-slice_bitcast_fusion.2
  176.9 4.1 %gather_fusion = f32[28,128,128]{2,1,0:T(8,128)} fusion(f32[16,4,128,128]{3,2,1,0:T(8,128)} %get-tuple-element.172, s32[28]{0:T(128)S(1)} %reshape.212), kind=kCustom, calls=%fused_computation.1.clone.1 | custom fusion | bytes 3670240 | tf_op jit(solution)/shard_map/while/body/eval_jaxpr/gather | solution.py:19
  181.1 4.2 %fusion.22 = f32[16,4,128,128]{3,2,1,0:T(8,128)} fusion(f32[16,4,128,128]{3,2,1,0:T(8,128)} %get-tuple-element.161, s32[]{:T(128)} %get-tuple-element.160, f32[4,7,128,128]{3,2,1,0:T(8,128)} %bitcast.62, f32[4,7,128,128]{3,2,1,0:T(8,128)S(1)} %bitcast.61, f32[4,7]{1,0:T(4,128)S(1)} %convert_bitcast_fusion.2), kind=kOutput, calls=%fused_computation.5.clone.1 | convolution fusion | flops 705101824 | bytes 3932784 | tf_op jit(solution)/shard_map/while/body/eval_jaxpr/omij,omjk->oik/dot_general | solution.py:20
  185.4 1.0 dynamic-slice_bitcast_fusion.2
  187.1 4.1 %gather_fusion = f32[28,128,128]{2,1,0:T(8,128)} fusion(f32[16,4,128,128]{3,2,1,0:T(8,128)} %get-tuple-element.172, s32[28]{0:T(128)S(1)} %reshape.212), kind=kCustom, calls=%fused_computation.1.clone.1 | custom fusion | bytes 3670240 | tf_op jit(solution)/shard_map/while/body/eval_jaxpr/gather | solution.py:19
  191.3 4.2 %fusion.22 = f32[16,4,128,128]{3,2,1,0:T(8,128)} fusion(f32[16,4,128,128]{3,2,1,0:T(8,128)} %get-tuple-element.161, s32[]{:T(128)} %get-tuple-element.160, f32[4,7,128,128]{3,2,1,0:T(8,128)} %bitcast.62, f32[4,7,128,128]{3,2,1,0:T(8,128)S(1)} %bitcast.61, f32[4,7]{1,0:T(4,128)S(1)} %convert_bitcast_fusion.2), kind=kOutput, calls=%fused_computation.5.clone.1 | convolution fusion | flops 705101824 | bytes 3932784 | tf_op jit(solution)/shard_map/while/body/eval_jaxpr/omij,omjk->oik/dot_general | solution.py:20
  195.6 1.0 dynamic-slice_bitcast_fusion.2
  197.4 4.1 %gather_fusion = f32[28,128,128]{2,1,0:T(8,128)} fusion(f32[16,4,128,128]{3,2,1,0:T(8,128)} %get-tuple-element.172, s32[28]{0:T(128)S(1)} %reshape.212), kind=kCustom, calls=%fused_computation.1.clone.1 | custom fusion | bytes 3670240 | tf_op jit(solution)/shard_map/while/body/eval_jaxpr/gather | solution.py:19
  201.5 4.2 %fusion.22 = f32[16,4,128,128]{3,2,1,0:T(8,128)} fusion(f32[16,4,128,128]{3,2,1,0:T(8,128)} %get-tuple-element.161, s32[]{:T(128)} %get-tuple-element.160, f32[4,7,128,128]{3,2,1,0:T(8,128)} %bitcast.62, f32[4,7,128,128]{3,2,1,0:T(8,128)S(1)} %bitcast.61, f32[4,7]{1,0:T(4,128)S(1)} %convert_bitcast_fusion.2), kind=kOutput, calls=%fused_computation.5.clone.1 | convolution fusion | flops 705101824 | bytes 3932784 | tf_op jit(solution)/shard_map/while/body/eval_jaxpr/omij,omjk->oik/dot_general | solution.py:20
  205.9 1.0 dynamic-slice_bitcast_fusion.2
  207.6 4.1 %gather_fusion = f32[28,128,128]{2,1,0:T(8,128)} fusion(f32[16,4,128,128]{3,2,1,0:T(8,128)} %get-tuple-element.172, s32[28]{0:T(128)S(1)} %reshape.212), kind=kCustom, calls=%fused_computation.1.clone.1 | custom fusion | bytes 3670240 | tf_op jit(solution)/shard_map/while/body/eval_jaxpr/gather | solution.py:19
  211.7 4.2 %fusion.22 = f32[16,4,128,128]{3,2,1,0:T(8,128)} fusion(f32[16,4,128,128]{3,2,1,0:T(8,128)} %get-tuple-element.161, s32[]{:T(128)} %get-tuple-element.160, f32[4,7,128,128]{3,2,1,0:T(8,128)} %bitcast.62, f32[4,7,128,128]{3,2,1,0:T(8,128)S(1)} %bitcast.61, f32[4,7]{1,0:T(4,128)S(1)} %convert_bitcast_fusion.2), kind=kOutput, calls=%fused_computation.5.clone.1 | convolution fusion | flops 705101824 | bytes 3932784 | tf_op jit(solution)/shard_map/while/body/eval_jaxpr/omij,omjk->oik/dot_general | solution.py:20
  216.1 1.0 dynamic-slice_bitcast_fusion.2
  217.8 4.1 %gather_fusion = f32[28,128,128]{2,1,0:T(8,128)} fusion(f32[16,4,128,128]{3,2,1,0:T(8,128)} %get-tuple-element.172, s32[28]{0:T(128)S(1)} %reshape.212), kind=kCustom, calls=%fused_computation.1.clone.1 | custom fusion | bytes 3670240 | tf_op jit(solution)/shard_map/while/body/eval_jaxpr/gather | solution.py:19
  221.9 4.2 %fusion.22 = f32[16,4,128,128]{3,2,1,0:T(8,128)} fusion(f32[16,4,128,128]{3,2,1,0:T(8,128)} %get-tuple-element.161, s32[]{:T(128)} %get-tuple-element.160, f32[4,7,128,128]{3,2,1,0:T(8,128)} %bitcast.62, f32[4,7,128,128]{3,2,1,0:T(8,128)S(1)} %bitcast.61, f32[4,7]{1,0:T(4,128)S(1)} %convert_bitcast_fusion.2), kind=kOutput, calls=%fused_computation.5.clone.1 | convolution fusion | flops 705101824 | bytes 3932784 | tf_op jit(solution)/shard_map/while/body/eval_jaxpr/omij,omjk->oik/dot_general | solution.py:20
  228.0 4.1 %gather_fusion = f32[28,128,128]{2,1,0:T(8,128)} fusion(f32[16,4,128,128]{3,2,1,0:T(8,128)} %get-tuple-element.172, s32[28]{0:T(128)S(1)} %reshape.212), kind=kCustom, calls=%fused_computation.1.clone.1 | custom fusion | bytes 3670240 | tf_op jit(solution)/shard_map/while/body/eval_jaxpr/gather | solution.py:19
  232.1 4.2 %fusion.22 = f32[16,4,128,128]{3,2,1,0:T(8,128)} fusion(f32[16,4,128,128]{3,2,1,0:T(8,128)} %get-tuple-element.161, s32[]{:T(128)} %get-tuple-element.160, f32[4,7,128,128]{3,2,1,0:T(8,128)} %bitcast.62, f32[4,7,128,128]{3,2,1,0:T(8,128)S(1)} %bitcast.61, f32[4,7]{1,0:T(4,128)S(1)} %convert_bitcast_fusion.2), kind=kOutput, calls=%fused_computation.5.clone.1 | convolution fusion | flops 705101824 | bytes 3932784 | tf_op jit(solution)/shard_map/while/body/eval_jaxpr/omij,omjk->oik/dot_general | solution.py:20
  236.5 1.0 dynamic-slice_bitcast_fusion.2
  238.2 4.1 %gather_fusion = f32[28,128,128]{2,1,0:T(8,128)} fusion(f32[16,4,128,128]{3,2,1,0:T(8,128)} %get-tuple-element.172, s32[28]{0:T(128)S(1)} %reshape.212), kind=kCustom, calls=%fused_computation.1.clone.1 | custom fusion | bytes 3670240 | tf_op jit(solution)/shard_map/while/body/eval_jaxpr/gather | solution.py:19
  242.3 4.2 %fusion.22 = f32[16,4,128,128]{3,2,1,0:T(8,128)} fusion(f32[16,4,128,128]{3,2,1,0:T(8,128)} %get-tuple-element.161, s32[]{:T(128)} %get-tuple-element.160, f32[4,7,128,128]{3,2,1,0:T(8,128)} %bitcast.62, f32[4,7,128,128]{3,2,1,0:T(8,128)S(1)} %bitcast.61, f32[4,7]{1,0:T(4,128)S(1)} %convert_bitcast_fusion.2), kind=kOutput, calls=%fused_computation.5.clone.1 | convolution fusion | flops 705101824 | bytes 3932784 | tf_op jit(solution)/shard_map/while/body/eval_jaxpr/omij,omjk->oik/dot_general | solution.py:20
  248.4 4.1 %gather_fusion = f32[28,128,128]{2,1,0:T(8,128)} fusion(f32[16,4,128,128]{3,2,1,0:T(8,128)} %get-tuple-element.172, s32[28]{0:T(128)S(1)} %reshape.212), kind=kCustom, calls=%fused_computation.1.clone.1 | custom fusion | bytes 3670240 | tf_op jit(solution)/shard_map/while/body/eval_jaxpr/gather | solution.py:19
  252.5 4.2 %fusion.22 = f32[16,4,128,128]{3,2,1,0:T(8,128)} fusion(f32[16,4,128,128]{3,2,1,0:T(8,128)} %get-tuple-element.161, s32[]{:T(128)} %get-tuple-element.160, f32[4,7,128,128]{3,2,1,0:T(8,128)} %bitcast.62, f32[4,7,128,128]{3,2,1,0:T(8,128)S(1)} %bitcast.61, f32[4,7]{1,0:T(4,128)S(1)} %convert_bitcast_fusion.2), kind=kOutput, calls=%fused_computation.5.clone.1 | convolution fusion | flops 705101824 | bytes 3932784 | tf_op jit(solution)/shard_map/while/body/eval_jaxpr/omij,omjk->oik/dot_general | solution.py:20
  256.9 1.0 dynamic-slice_bitcast_fusion.2
  258.6 4.1 %gather_fusion = f32[28,128,128]{2,1,0:T(8,128)} fusion(f32[16,4,128,128]{3,2,1,0:T(8,128)} %get-tuple-element.172, s32[28]{0:T(128)S(1)} %reshape.212), kind=kCustom, calls=%fused_computation.1.clone.1 | custom fusion | bytes 3670240 | tf_op jit(solution)/shard_map/while/body/eval_jaxpr/gather | solution.py:19
  262.7 4.2 %fusion.22 = f32[16,4,128,128]{3,2,1,0:T(8,128)} fusion(f32[16,4,128,128]{3,2,1,0:T(8,128)} %get-tuple-element.161, s32[]{:T(128)} %get-tuple-element.160, f32[4,7,128,128]{3,2,1,0:T(8,128)} %bitcast.62, f32[4,7,128,128]{3,2,1,0:T(8,128)S(1)} %bitcast.61, f32[4,7]{1,0:T(4,128)S(1)} %convert_bitcast_fusion.2), kind=kOutput, calls=%fused_computation.5.clone.1 | convolution fusion | flops 705101824 | bytes 3932784 | tf_op jit(solution)/shard_map/while/body/eval_jaxpr/omij,omjk->oik/dot_general | solution.py:20
  268.8 4.1 %gather_fusion = f32[28,128,128]{2,1,0:T(8,128)} fusion(f32[16,4,128,128]{3,2,1,0:T(8,128)} %get-tuple-element.172, s32[28]{0:T(128)S(1)} %reshape.212), kind=kCustom, calls=%fused_computation.1.clone.1 | custom fusion | bytes 3670240 | tf_op jit(solution)/shard_map/while/body/eval_jaxpr/gather | solution.py:19
  272.9 4.2 %fusion.22 = f32[16,4,128,128]{3,2,1,0:T(8,128)} fusion(f32[16,4,128,128]{3,2,1,0:T(8,128)} %get-tuple-element.161, s32[]{:T(128)} %get-tuple-element.160, f32[4,7,128,128]{3,2,1,0:T(8,128)} %bitcast.62, f32[4,7,128,128]{3,2,1,0:T(8,128)S(1)} %bitcast.61, f32[4,7]{1,0:T(4,128)S(1)} %convert_bitcast_fusion.2), kind=kOutput, calls=%fused_computation.5.clone.1 | convolution fusion | flops 705101824 | bytes 3932784 | tf_op jit(solution)/shard_map/while/body/eval_jaxpr/omij,omjk->oik/dot_general | solution.py:20
  277.3 1.0 dynamic-slice_bitcast_fusion.2
  279.0 4.1 %gather_fusion = f32[28,128,128]{2,1,0:T(8,128)} fusion(f32[16,4,128,128]{3,2,1,0:T(8,128)} %get-tuple-element.172, s32[28]{0:T(128)S(1)} %reshape.212), kind=kCustom, calls=%fused_computation.1.clone.1 | custom fusion | bytes 3670240 | tf_op jit(solution)/shard_map/while/body/eval_jaxpr/gather | solution.py:19
  283.2 4.2 %fusion.22 = f32[16,4,128,128]{3,2,1,0:T(8,128)} fusion(f32[16,4,128,128]{3,2,1,0:T(8,128)} %get-tuple-element.161, s32[]{:T(128)} %get-tuple-element.160, f32[4,7,128,128]{3,2,1,0:T(8,128)} %bitcast.62, f32[4,7,128,128]{3,2,1,0:T(8,128)S(1)} %bitcast.61, f32[4,7]{1,0:T(4,128)S(1)} %convert_bitcast_fusion.2), kind=kOutput, calls=%fused_computation.5.clone.1 | convolution fusion | flops 705101824 | bytes 3932784 | tf_op jit(solution)/shard_map/while/body/eval_jaxpr/omij,omjk->oik/dot_general | solution.py:20
  287.5 1.0 dynamic-slice_bitcast_fusion.2
  289.2 4.1 %gather_fusion = f32[28,128,128]{2,1,0:T(8,128)} fusion(f32[16,4,128,128]{3,2,1,0:T(8,128)} %get-tuple-element.172, s32[28]{0:T(128)S(1)} %reshape.212), kind=kCustom, calls=%fused_computation.1.clone.1 | custom fusion | bytes 3670240 | tf_op jit(solution)/shard_map/while/body/eval_jaxpr/gather | solution.py:19
  293.4 4.2 %fusion.22 = f32[16,4,128,128]{3,2,1,0:T(8,128)} fusion(f32[16,4,128,128]{3,2,1,0:T(8,128)} %get-tuple-element.161, s32[]{:T(128)} %get-tuple-element.160, f32[4,7,128,128]{3,2,1,0:T(8,128)} %bitcast.62, f32[4,7,128,128]{3,2,1,0:T(8,128)S(1)} %bitcast.61, f32[4,7]{1,0:T(4,128)S(1)} %convert_bitcast_fusion.2), kind=kOutput, calls=%fused_computation.5.clone.1 | convolution fusion | flops 705101824 | bytes 3932784 | tf_op jit(solution)/shard_map/while/body/eval_jaxpr/omij,omjk->oik/dot_general | solution.py:20
  297.7 1.0 dynamic-slice_bitcast_fusion.2
  299.4 4.1 %gather_fusion = f32[28,128,128]{2,1,0:T(8,128)} fusion(f32[16,4,128,128]{3,2,1,0:T(8,128)} %get-tuple-element.172, s32[28]{0:T(128)S(1)} %reshape.212), kind=kCustom, calls=%fused_computation.1.clone.1 | custom fusion | bytes 3670240 | tf_op jit(solution)/shard_map/while/body/eval_jaxpr/gather | solution.py:19
  303.6 4.2 %fusion.22 = f32[16,4,128,128]{3,2,1,0:T(8,128)} fusion(f32[16,4,128,128]{3,2,1,0:T(8,128)} %get-tuple-element.161, s32[]{:T(128)} %get-tuple-element.160, f32[4,7,128,128]{3,2,1,0:T(8,128)} %bitcast.62, f32[4,7,128,128]{3,2,1,0:T(8,128)S(1)} %bitcast.61, f32[4,7]{1,0:T(4,128)S(1)} %convert_bitcast_fusion.2), kind=kOutput, calls=%fused_computation.5.clone.1 | convolution fusion | flops 705101824 | bytes 3932784 | tf_op jit(solution)/shard_map/while/body/eval_jaxpr/omij,omjk->oik/dot_general | solution.py:20
  307.9 1.0 dynamic-slice_bitcast_fusion.2
  309.6 4.1 %gather_fusion = f32[28,128,128]{2,1,0:T(8,128)} fusion(f32[16,4,128,128]{3,2,1,0:T(8,128)} %get-tuple-element.172, s32[28]{0:T(128)S(1)} %reshape.212), kind=kCustom, calls=%fused_computation.1.clone.1 | custom fusion | bytes 3670240 | tf_op jit(solution)/shard_map/while/body/eval_jaxpr/gather | solution.py:19
  313.8 4.2 %fusion.22 = f32[16,4,128,128]{3,2,1,0:T(8,128)} fusion(f32[16,4,128,128]{3,2,1,0:T(8,128)} %get-tuple-element.161, s32[]{:T(128)} %get-tuple-element.160, f32[4,7,128,128]{3,2,1,0:T(8,128)} %bitcast.62, f32[4,7,128,128]{3,2,1,0:T(8,128)S(1)} %bitcast.61, f32[4,7]{1,0:T(4,128)S(1)} %convert_bitcast_fusion.2), kind=kOutput, calls=%fused_computation.5.clone.1 | convolution fusion | flops 705101824 | bytes 3932784 | tf_op jit(solution)/shard_map/while/body/eval_jaxpr/omij,omjk->oik/dot_general | solution.py:20
  319.8 4.1 %gather_fusion = f32[28,128,128]{2,1,0:T(8,128)} fusion(f32[16,4,128,128]{3,2,1,0:T(8,128)} %get-tuple-element.172, s32[28]{0:T(128)S(1)} %reshape.212), kind=kCustom, calls=%fused_computation.1.clone.1 | custom fusion | bytes 3670240 | tf_op jit(solution)/shard_map/while/body/eval_jaxpr/gather | solution.py:19
  324.0 4.2 %fusion.22 = f32[16,4,128,128]{3,2,1,0:T(8,128)} fusion(f32[16,4,128,128]{3,2,1,0:T(8,128)} %get-tuple-element.161, s32[]{:T(128)} %get-tuple-element.160, f32[4,7,128,128]{3,2,1,0:T(8,128)} %bitcast.62, f32[4,7,128,128]{3,2,1,0:T(8,128)S(1)} %bitcast.61, f32[4,7]{1,0:T(4,128)S(1)} %convert_bitcast_fusion.2), kind=kOutput, calls=%fused_computation.5.clone.1 | convolution fusion | flops 705101824 | bytes 3932784 | tf_op jit(solution)/shard_map/while/body/eval_jaxpr/omij,omjk->oik/dot_general | solution.py:20
  328.2 60.0 %reduce-scatter.2.cloned.1.call-done = f32[8,4,128,128]{3,2,1,0:T(8,128)} async-done(((f32[16,4,128,128]{3,2,1,0:T(8,128)}), f32[8,4,128,128]{3,2,1,0:T(8,128)}) %reduce-scatter.2.cloned.1.call-update) | async-done | bytes 2097168 | tf_op jit(solution)/shard_map/reduce_scatter | solution.py:24
  (125 shorter events, 21.8 us)
Async XLA Ops:
  6.5 53.2 %all-gather.3.cloned.1.call-start = ((), (), s32[]{:S(2)}) async-start(), calls=%async_computation.1 | async-start | bytes 4456448 | tf_op jit(solution)/shard_map/all_gather | solution.py:22
  7.3 157.5 %all-gather.5.cloned.1.call-start = ((), (), s32[]{:S(2)}) async-start(), calls=%async_computation.2 | async-start | bytes 4456448 | tf_op jit(solution)/shard_map/all_gather | solution.py:11
  8.0 380.1 %reduce-scatter.2.cloned.1.call-start = ((), (), s32[]{:S(2)}) async-start(), calls=%async_computation.3 | async-start | bytes 6291456 | tf_op jit(solution)/shard_map/reduce_scatter | solution.py:24
Sparse Core Ops, SparseCore 0:
  9.5 50.2 all-gather.2
  62.9 101.8 all-gather.4
  328.3 59.8 reduce-scatter.1
where the time goes:
time: 398 us; the launch traced here: 395 us
  waiting for transfers between devices  217 us (55%)
  local copies, waits for them, and re-layouts  96.4 us (24%)
  matrix products  66.8 us (17%)
  between operations  13.1 us (3%)
    all_gather x1, waiting for transfers between devices, shards(): p_panel = lax.all_gather(p_blocks, 'row', axis=0, tiled=True)  105 us
    dot_general x16, matrix products, row_work(): jnp.einsum('omij,omjk->oik', a_sel, p_sel, precision=lax.Precision.HIGHEST)  66.8 us
    gather x16, local copies, waits for them, and re-layouts, row_work(): p_sel = p_panel[out_cols[:, None], p_pick]  66 us
    reduce_scatter x1, waiting for transfers between devices, shards(): lax.psum_scatter(partial_value, 'layer', scatter_dimension=0, tiled=True)  60 us
    all_gather x1, waiting for transfers between devices, shards(): a_panel = lax.all_gather(a_blocks, 'col', axis=0, tiled=True)  50.1 us
    squeeze x16, local copies, waits for them, and re-layouts, shards(): partial_value = lax.map(row_work, (a_panel, out_columns, pair_codes))  15.5 us
    gather x16, local copies, waits for them, and re-layouts, row_work(): a_sel = a_row[a_pick] * is_live[:, :, None, None].astype(jnp.float32)  10.7 us
  transfers between devices with their start and end apart: 3, of which 3 were waited for; matrix products, arithmetic and copies ran while one was open for 0% of the time, Pallas kernels for 0%

commit v1 on v0

v1 whole, which is shorter than its diff:
```python
import jax
import jax.numpy as jnp
from jax import lax
from jax.experimental import pallas as pl
from jax.experimental.pallas import tpu as pltpu
from jax.sharding import PartitionSpec as P

MESH = pl.DeviceIdType.MESH
BS = 128
SLOTS = 4
DEPTH = SLOTS * BS
MP = 7
NX, NY, NZ = 4, 8, 8
R1 = 224
GROUP = {1: (0, R1), 2: (R1, DEPTH - R1)}
RATE = 100e3
LAG = 1.5
FAR, NEAR = 5, 2


def onward(g, a, b):
    out = []
    if g == 1:
        if b == 0:
            if a == 0:
                out += [(1, 0, "x", 1), (-1, 0, "x", -1)]
            if a == 1:
                out += [(2, 0, "x", 1)]
            out += [(a, 1, "y", 1), (a, -1, "y", -1)]
        elif 0 < b < 4:
            out += [(a, b + 1, "y", 1)]
        elif -3 < b < 0:
            out += [(a, b - 1, "y", -1)]
    else:
        if a == 0:
            if b == 0:
                out += [(0, 1, "y", 1), (0, -1, "y", -1)]
            elif 0 < b < 4:
                out += [(0, b + 1, "y", 1)]
            elif -3 < b < 0:
                out += [(0, b - 1, "y", -1)]
            out += [(1, b, "x", 1), (-1, b, "x", -1)]
        elif a == 1:
            out += [(2, b, "x", 1)]
    return out


def arrivals():
    free = {"x": 0.0, "y": 0.0}
    queue = []
    count = 0

    def push(at, g, a, b):
        nonlocal count
        for a2, b2, axis, _ in onward(g, a, b):
            count += 1
            queue.append((at, count, g, a2, b2, axis))

    push(0.0, 2, 0, 0)
    push(0.0, 1, 0, 0)
    order = []
    while queue:
        queue.sort()
        at, _, g, a, b, axis = queue.pop(0)
        free[axis] = max(at, free[axis]) + GROUP[g][1] * BS * 4 / RATE
        order.append((free[axis] + LAG, (g, a, b)))
        push(free[axis] + LAG + 0.1, g, a, b)
    return sorted(order)


def kernel(
    a_ref, p_ref, cols_ref, codes_ref, out_ref,
    p_own, p_opp, ps_own, ps_opp, a_own, a_opp, b_own, b_opp, codes_own, codes_opp,
    p_recv, p_send, a_recv, a_send, sib_recv, sib_send, swap_send, codes_sem, local_sem,
):
    row, col, layer = lax.axis_index("row"), lax.axis_index("col"), lax.axis_index("layer")
    y, z, core = lax.rem(row, NY), col // 2, lax.rem(col, 2)
    x = (row // NY) * 2 + layer
    turn = 1 - 2 * core
    t = lax.rem(z + 2 * NZ - 4 * layer, NZ)
    q_me = row
    s_me = lax.rem(t, 4)

    def device(x_, y_, z_, core_):
        return ((x_ // 2) * NY + y_, z_ * 2 + core_, lax.rem(x_, 2))

    def along(axis, way):
        if axis == "x":
            return device(lax.rem(x + NX + turn * way, NX), y, z, core)
        if axis == "y":
            return device(x, lax.rem(y + NY + turn * way, NY), z, core)
        return device(x, y, lax.rem(z + NZ + way, NZ), core)

    sibling = device(x, y, z, 1 - core)
    partner = (row, col, 1 - layer)

    barrier = pltpu.get_barrier_semaphore()
    greeted = [along(axis, way) for axis in "xyz" for way in (1, -1)] + [sibling]
    for other in greeted:
        pl.semaphore_signal(barrier, inc=1, device_id=other, device_id_type=MESH)
    pl.semaphore_wait(barrier, len(greeted))

    p_land = (p_own, p_opp)
    p_split = (ps_own, ps_opp)
    a_land = (a_own, a_opp)
    b_parts = (b_own, b_opp)
    codes_land = (codes_own, codes_opp)

    def p_slot(a, b):
        x0 = lax.rem(x + 2 * NX - turn * a, NX)
        y0 = lax.rem(y + 2 * NY - turn * b, NY)
        return (x0 // 2) * NY + y0


    def p_piece(g, a, b):
        lo, size = GROUP[g]
        return p_land[a % 2].at[p_slot(a, b), pl.ds(lo, size)]

    def p_forward(g, a, b):
        lo, size = GROUP[g]
        src = p_ref.at[pl.ds(lo, size)] if (a, b) == (0, 0) else p_piece(g, a, b)
        copies = []
        for a2, b2, axis, way in onward(g, a, b):
            copies.append(
                pltpu.make_async_remote_copy(
                    src_ref=src,
                    dst_ref=p_land[a2 % 2].at[p_slot(a, b), pl.ds(lo, size)],
                    send_sem=p_send.at[g - 1, a2 + 1, b2 + 3],
                    recv_sem=p_recv.at[g - 1, a2 + 1, b2 + 3],
                    device_id=along(axis, way),
                    device_id_type=MESH,
                )
            )
        return copies

    def p_wait(g, a, b):
        here = p_piece(g, a, b)
        pltpu.make_async_remote_copy(
            src_ref=here,
            dst_ref=here,
            send_sem=p_send.at[g - 1, a + 1, b + 3],
            recv_sem=p_recv.at[g - 1, a + 1, b + 3],
            device_id=along("x", 1),
            device_id_type=MESH,
        ).wait_recv()

    def p_convert(a, b, lo, size):
        q = p_slot(a, b)
        value = p_land[a % 2][q, pl.ds(lo, size), :]
        high = value.astype(jnp.bfloat16)
        low = (value - high.astype(jnp.float32)).astype(jnp.bfloat16)
        p_split[a % 2][q, pl.ds(lo, size), pl.ds(0, BS)] = high
        p_split[a % 2][q, pl.ds(lo, size), pl.ds(BS, BS)] = low

    half = DEPTH // 2

    def a_rows(which, s, h):
        return a_land[which].at[2 * s + core, pl.ds(h * half, half)]

    def a_copy(which, h, s, d, way, src):
        return pltpu.make_async_remote_copy(
            src_ref=src,
            dst_ref=a_rows(which, s, h),
            send_sem=a_send.at[which, h, (1 - way) // 2, d],
            recv_sem=a_recv.at[which, h, s],
            device_id=along("z", way),
            device_id_type=MESH,
        )

    def a_wait(which, h, s):
        here = a_rows(which, s, h)
        pltpu.make_async_remote_copy(
            src_ref=here,
            dst_ref=here,
            send_sem=a_send.at[which, h, 0, 0],
            recv_sem=a_recv.at[which, h, s],
            device_id=along("z", 1),
            device_id_type=MESH,
        ).wait_recv()

    def sib_copy(which, s, src=None):
        here = a_land[which].at[2 * s + core]
        return pltpu.make_async_remote_copy(
            src_ref=here if src is None else src,
            dst_ref=here,
            send_sem=sib_send.at[which, s],
            recv_sem=sib_recv.at[which, s],
            device_id=sibling,
            device_id_type=MESH,
        )

    def sib_wait(which, s):
        there = a_land[which].at[2 * s + 1 - core]
        pltpu.make_async_remote_copy(
            src_ref=there,
            dst_ref=there,
            send_sem=sib_send.at[which, s],
            recv_sem=sib_recv.at[which, s],
            device_id=sibling,
            device_id_type=MESH,
        ).wait_recv()

    def swap_copy(h):
        return pltpu.make_async_remote_copy(
            src_ref=a_ref.at[pl.ds(h * half, half)],
            dst_ref=a_opp.at[2 * s_me + core, pl.ds(h * half, half)],
            send_sem=swap_send.at[h],
            recv_sem=a_recv.at[1, h, s_me],
            device_id=partner,
            device_id_type=MESH,
        )

    def moving(d, way):
        s = lax.rem(t + 2 * NZ - way * d, NZ)
        far = jnp.logical_and(s >= 2, s < 4) if way == 1 else s < 2
        valid = far if d > NEAR else s < 4
        goes_on = jnp.logical_and(valid, far) if d >= NEAR else valid
        if d == FAR:
            goes_on = None
        return lax.rem(s, 4), valid, goes_on

    codes_own[...] = jnp.full(codes_own.shape, SLOTS * SLOTS, jnp.int32)
    codes_own[:, pl.ds(0, SLOTS), pl.ds(0, MP)] = codes_ref[...]
    codes_copy = pltpu.make_async_remote_copy(
        src_ref=codes_own.at[pl.ds(8 * (1 - layer), 8)],
        dst_ref=codes_opp,
        send_sem=codes_sem.at[0],
        recv_sem=codes_sem.at[1],
        device_id=partner,
        device_id_type=MESH,
    )

    def combine(which, s):
        def step(i, carry):
            r, o = 2 * s + i // SLOTS, lax.rem(i, SLOTS)
            code_row = 8 * layer + r if which == 0 else r
            codes = codes_land[which][code_row, pl.ds(o, 1), :]
            index = lax.broadcasted_iota(jnp.int32, (SLOTS * SLOTS, BS), 0)
            live = jnp.zeros((SLOTS * SLOTS, BS), jnp.float32)
            for m in range(MP):
                live += (codes[:, m : m + 1] == index).astype(jnp.float32)
            strip = 32
            for k in range(BS // strip):
                parts = [a_land[which][r, pl.ds(a * BS + k * strip, strip), :] for a in range(SLOTS)]
                for p in range(SLOTS):
                    total = parts[0] * live[p : p + 1]
                    for a in range(1, SLOTS):
                        total += parts[a] * live[a * SLOTS + p : a * SLOTS + p + 1]
                    high = total.astype(jnp.bfloat16)
                    low = (total - high.astype(jnp.float32)).astype(jnp.bfloat16)
                    b_parts[which][r * SLOTS + o, pl.ds(k * strip, strip), pl.ds(p * BS, BS)] = high
                    b_parts[which][r * SLOTS + o, pl.ds(BS + k * strip, strip), pl.ds(p * BS, BS)] = low
            return carry

        lax.fori_loop(0, 2 * SLOTS, step, 0)

    def products(which):
        unroll = 4

        def step(i, carry):
            for j in range(unroll):
                o = i * unroll + j
                q = cols_ref[8 * layer + o // SLOTS, lax.rem(o, SLOTS)]
                four = jnp.dot(b_parts[which][o], p_split[which][q], preferred_element_type=jnp.float32)
                value = (four[BS:, BS:] + four[:BS, BS:] + four[BS:, :BS]) + four[:BS, :BS]
                out_ref[o] = value if which == 1 else out_ref[o] + value
            return carry

        lax.fori_loop(0, 8 * SLOTS // unroll, step, 0)

    events = []
    started = []

    def add(at, act):
        events.append((at, len(events), act))

    p_local = pltpu.make_async_copy(p_ref, p_own.at[q_me], local_sem.at[0])
    a_local = pltpu.make_async_copy(a_ref, a_own.at[2 * s_me + core], local_sem.at[1])

    def start():
        for copy in p_forward(2, 0, 0) + p_forward(1, 0, 0):
            copy.start()

        @pl.when(t < 4)
        def _():
            for h in range(2):
                for way in (1, -1):
                    a_copy(0, h, s_me, 0, way, a_ref.at[pl.ds(h * half, half)]).start()
            a_local.start()
            sib_copy(0, s_me, a_ref).start()

        @pl.when(t >= 4)
        def _():
            for h in range(2):
                swap_copy(h).start()

        codes_copy.start()
        p_local.start()

    def own_convert():
        p_local.wait()
        p_convert(0, 0, 0, DEPTH)

    def codes_arrive():
        codes_copy.wait()

    add(0.0, start)
    add(2.0, own_convert)
    add(2.5, codes_arrive)

    def p_event(g, a, b):
        def act():
            p_wait(g, a, b)
            for copy in p_forward(g, a, b):
                copy.start()
            p_convert(a, b, *GROUP[g])

        return act

    planned = arrivals()
    for at, (g, a, b) in planned:
        add(at, p_event(g, a, b))
    opp_done = max(at for at, (g, a, b) in planned if a % 2)
    last_sent = max(at for at, (g, a, b) in planned if onward(g, a, b))
    last = max(at for at, _ in planned)

    def self_event(which, h):
        def act():
            @pl.when(t < 4)
            def _():
                a_wait(1, h, s_me)
                for way in (1, -1):
                    a_copy(1, h, s_me, 0, way, a_rows(1, s_me, h)).start()
                if h == 1:
                    sib_copy(1, s_me).start()

        return act

    def self_combine(which):
        def act():
            @pl.when(t < 4)
            def _():
                if which == 0:
                    a_local.wait()
                sib_wait(which, s_me)
                combine(which, s_me)

        return act

    def hop_event(which, h, d, way):
        def act():
            s, valid, goes_on = moving(d, way)

            @pl.when(valid)
            def _():
                a_wait(which, h, s)
                if goes_on is not None:

                    @pl.when(goes_on)
                    def _():
                        a_copy(which, h, s, d, way, a_rows(which, s, h)).start()

                if h == 1:
                    sib_copy(which, s).start()

        return act

    def hop_combine(which, d, way):
        def act():
            s, valid, _ = moving(d, way)

            @pl.when(valid)
            def _():
                sib_wait(which, s)
                combine(which, s)

        return act

    for h in range(2):
        add(7.0 + 2.6 * h, self_event(1, h))
    add(5.0, self_combine(0))
    add(14.0, self_combine(1))
    for which in range(2):
        for d in range(1, FAR + 1):
            for h in range(2):
                at = 4.0 + 4.2 * d + 2.6 * h + 10.0 * which
                for way in (1, -1):
                    add(at, hop_event(which, h, d, way))
            for way in (1, -1):
                add(at + 3.0, hop_combine(which, d, way))
    b_opp_done = at + 3.0

    add(max(max(opp_done, last_sent), b_opp_done) + 0.05, lambda: products(1))
    add(max(last, b_opp_done) + 0.1, lambda: products(0))

    for _, _, act in sorted(events, key=lambda e: e[:2]):
        act()

    for g in (1, 2):
        for a in range(-1, 3):
            for b in range(-3, 5):
                for copy in p_forward(g, a, b):
                    copy.wait_send()

    @pl.when(t < 4)
    def _():
        for which in range(2):
            for h in range(2):
                for way in (1, -1):
                    a_copy(which, h, s_me, 0, way, a_rows(which, s_me, h)).wait_send()
            sib_copy(which, s_me).wait_send()

    @pl.when(t >= 4)
    def _():
        for h in range(2):
            swap_copy(h).wait_send()

    for which in range(2):
        for d in range(1, FAR + 1):
            for way in (1, -1):
                s, valid, goes_on = moving(d, way)

                @pl.when(valid)
                def _():
                    sib_copy(which, s).wait_send()

                if goes_on is not None:

                    @pl.when(goes_on)
                    def _():
                        for h in range(2):
                            a_copy(which, h, s, d, way, a_rows(which, s, h)).wait_send()


def shards(a_blocks, p_blocks, out_columns, pair_codes):
    vmem, smem, anywhere = pltpu.VMEM, pltpu.SMEM, pl.ANY
    dma = pltpu.SemaphoreType.DMA
    f32, bf16 = jnp.float32, jnp.bfloat16
    product = pl.pallas_call(
        kernel,
        out_shape=jax.ShapeDtypeStruct((8 * SLOTS, BS, BS), f32),
        in_specs=[
            pl.BlockSpec(memory_space=anywhere),
            pl.BlockSpec(memory_space=anywhere),
            pl.BlockSpec(memory_space=smem),
            pl.BlockSpec(memory_space=vmem),
        ],
        out_specs=pl.BlockSpec(memory_space=vmem),
        scratch_shapes=[
            vmem((16, DEPTH, BS), f32),
            vmem((16, DEPTH, BS), f32),
            vmem((16, DEPTH, 2 * BS), bf16),
            vmem((16, DEPTH, 2 * BS), bf16),
            vmem((8, DEPTH, BS), f32),
            vmem((8, DEPTH, BS), f32),
            vmem((8 * SLOTS, 2 * BS, DEPTH), bf16),
            vmem((8 * SLOTS, 2 * BS, DEPTH), bf16),
            vmem((16, 8, BS), jnp.int32),
            vmem((8, 8, BS), jnp.int32),
            dma((2, 4, 8)),
            dma((2, 4, 8)),
            dma((2, 2, 4)),
            dma((2, 2, 2, FAR + 1)),
            dma((2, 4)),
            dma((2, 4)),
            dma((2,)),
            dma((2,)),
            dma((2,)),
        ],
        compiler_params=pltpu.CompilerParams(
            collective_id=0, has_side_effects=True, vmem_limit_bytes=56 * 2**20
        ),
        cost_estimate=pl.CostEstimate(flops=4 * 10**9, bytes_accessed=5 * 2**20, transcendentals=0),
    )(
        a_blocks.reshape(DEPTH, BS),
        p_blocks.reshape(DEPTH, BS),
        out_columns,
        pair_codes,
    )
    return product.reshape(8, SLOTS, BS, BS)


def solution(mesh):
    return jax.shard_map(
        shards,
        mesh=mesh,
        in_specs=(
            P(("row", "col"), "layer", None, None),
            P(("row", "col"), "layer", None, None),
            P("row", "col"),
            P("row", "col", "layer"),
        ),
        out_specs=P(("row", "layer"), "col", None, None),
        check_vma=False,
    )
```

time: 398 us -> 91.4 us (0.23)
  waiting for transfers between devices: 217 us -> 0 us
  local copies, waits for them, and re-layouts: 96.4 us -> 5.91 us
  Pallas kernels: 0 us -> 83.9 us
  matrix products: 66.8 us -> 0 us
  between operations: 13.1 us -> 0.01 us
    all_gather x2 -> x0, waiting for transfers between devices: 155 us -> none  [the longest x1 105 us: shards(): p_panel = lax.all_gather(p_blocks, 'row', axis=0, tiled=True)]
    pallas_call x0 -> x1, Pallas kernels: none -> 83.9 us  [shards(): pl.pallas_call(kernel, out_shape=jax.ShapeDtypeStruct((8 * SLOTS, BS, BS)...]
    gather x32 -> x0, local copies, waits for them, and re-layouts: 76.6 us -> none  [the longest x16 66 us: row_work(): p_sel = p_panel[out_cols[:, None], p_pick]]
    dot_general x16 -> x0, matrix products: 66.8 us -> none  [row_work(): jnp.einsum('omij,omjk->oik', a_sel, p_sel, precision=lax.Precision.HIGHEST)]
    reduce_scatter x1 -> x0, waiting for transfers between devices: 60 us -> none  [shards(): lax.psum_scatter(partial_value, 'layer', scatter_dimension=0, tiled=True)]
    squeeze x16 -> x0, local copies, waits for them, and re-layouts: 15.5 us -> none  [shards(): partial_value = lax.map(row_work, (a_panel, out_columns, pair_codes))]
    unnamed x0 -> x3, local copies, waits for them, and re-layouts: none -> 5.91 us
  transfers between devices with their start and end apart: 3 -> 0, of which waited for: 3 -> 0; matrix products, arithmetic and copies ran while one was open for 0% -> 0% of each run, Pallas kernels for 0% -> 0%
where the time goes in v1:
time: 91.4 us; the launch traced here: 89.8 us
  Pallas kernels  83.9 us (92%)
  local copies, waits for them, and re-layouts  5.91 us (6%)
    pallas_call x1, Pallas kernels, shards(): pl.pallas_call(kernel, out_shape=jax.ShapeDtypeStruct((8 * SLOTS, BS, BS)...  83.9 us
    unnamed x3, local copies, waits for them, and re-layouts  5.91 us

profile of v1, /device:TPU:6, one launch (start us, length us, event | category | flops | bytes accessed | tf_op | source)
XLA Modules:
  0.0 89.8 jit_solution(1320607852631421030)
XLA Ops:
  0.0 1.4 %copy.5.cols_ref = s32[16,4]{1,0:T(8,128)} copy(s32[16,4]{0,1:T(4,128)} %param.6) | data formatting | bytes 512 | tf_op args[2]
  1.4 1.4 %copy.6.codes_ref = s32[16,4,7]{2,1,0:T(4,128)} copy(s32[16,4,7]{0,1,2:T(4,128)} %param.7) | data formatting | bytes 3584 | tf_op args[3]
  2.8 83.9 %shard_map.46 = f32[32,128,128]{2,1,0:T(8,128)} custom-call(f32[512,128]{1,0:T(8,128)} %bitcast.4, f32[512,128]{1,0:T(8,128)} %bitcast.5, s32[16,4]{1,0:T(8,128)} %copy.5.cols_ref, s32[16,4,7]{2,1,0:T(4,128)} %copy.6.codes_ref), custom_call_target="tpu_custom_call" | custom-call | flops 4000000000 | bytes 5242880 | tf_op jit(solution)/shard_map/pallas_call | solution.py:439
  86.7 3.1 %copy.8 = f32[8,4,128,128]{3,2,1,0:T(8,128)} copy(f32[8,4,128,128]{3,2,1,0:T(8,128)} %bitcast.3) | data formatting | bytes 4194304

commit v2 on v1

--- a/solution.py
+++ b/solution.py
@@ -70,7 +70,8 @@
 
 def kernel(
     a_ref, p_ref, cols_ref, codes_ref, out_ref,
-    p_own, p_opp, ps_own, ps_opp, a_own, a_opp, b_own, b_opp, codes_own, codes_opp,
+    p_own, p_opp, ps_own, ps_opp, a_own, a_opp, sums_own, sums_opp, codes_own, codes_opp,
+    picks_own, picks_opp, picks_smem_own, picks_smem_opp,
     p_recv, p_send, a_recv, a_send, sib_recv, sib_send, swap_send, codes_sem, local_sem,
 ):
     row, col, layer = lax.axis_index("row"), lax.axis_index("col"), lax.axis_index("layer")
@@ -103,7 +104,9 @@
     p_land = (p_own, p_opp)
     p_split = (ps_own, ps_opp)
     a_land = (a_own, a_opp)
-    b_parts = (b_own, b_opp)
+    sums = (sums_own, sums_opp)
+    picks = (picks_own, picks_opp)
+    picks_smem = (picks_smem_own, picks_smem_opp)
     codes_land = (codes_own, codes_opp)
 
     def p_slot(a, b):
@@ -220,9 +223,9 @@
         return lax.rem(s, 4), valid, goes_on
 
     codes_own[...] = jnp.full(codes_own.shape, SLOTS * SLOTS, jnp.int32)
-    codes_own[:, pl.ds(0, SLOTS), pl.ds(0, MP)] = codes_ref[...]
+    codes_own[:, pl.ds(0, SLOTS), pl.ds(0, 16)] = codes_ref[...]
     codes_copy = pltpu.make_async_remote_copy(
-        src_ref=codes_own.at[pl.ds(8 * (1 - layer), 8)],
+        src_ref=codes_own,
         dst_ref=codes_opp,
         send_sem=codes_sem.at[0],
         recv_sem=codes_sem.at[1],
@@ -230,43 +233,52 @@
         device_id_type=MESH,
     )
 
+    def pick_copy(which):
+        return pltpu.make_async_copy(picks[which], picks_smem[which], local_sem.at[2 + which])
+
+    def pick(which):
+        codes = [codes_land[which][m] for m in range(MP)]
+        for p in range(SLOTS):
+            total = jnp.zeros((8, BS), jnp.int32)
+            for code in codes:
+                for a in range(SLOTS):
+                    total += jnp.where(code == a * SLOTS + p, 1 << a, 0)
+            picks[which][p] = total
+        pick_copy(which).start()
+
     def combine(which, s):
         def step(i, carry):
-            r, o = 2 * s + i // SLOTS, lax.rem(i, SLOTS)
-            code_row = 8 * layer + r if which == 0 else r
-            codes = codes_land[which][code_row, pl.ds(o, 1), :]
-            index = lax.broadcasted_iota(jnp.int32, (SLOTS * SLOTS, BS), 0)
-            live = jnp.zeros((SLOTS * SLOTS, BS), jnp.float32)
-            for m in range(MP):
-                live += (codes[:, m : m + 1] == index).astype(jnp.float32)
-            strip = 32
+            r = 2 * s + i
+            strip = 16
             for k in range(BS // strip):
-                parts = [a_land[which][r, pl.ds(a * BS + k * strip, strip), :] for a in range(SLOTS)]
-                for p in range(SLOTS):
-                    total = parts[0] * live[p : p + 1]
-                    for a in range(1, SLOTS):
-                        total += parts[a] * live[a * SLOTS + p : a * SLOTS + p + 1]
-                    high = total.astype(jnp.bfloat16)
-                    low = (total - high.astype(jnp.float32)).astype(jnp.bfloat16)
-                    b_parts[which][r * SLOTS + o, pl.ds(k * strip, strip), pl.ds(p * BS, BS)] = high
-                    b_parts[which][r * SLOTS + o, pl.ds(BS + k * strip, strip), pl.ds(p * BS, BS)] = low
+                total = {0: None}
+                for n in range(1, 16):
+                    a = n.bit_length() - 1
+                    part = a_land[which][r, pl.ds(a * BS + k * strip, strip), :] if n == 1 << a else None
+                    total[n] = part if n == 1 << a else total[n - (1 << a)] + total[1 << a]
+                    high = total[n].astype(jnp.bfloat16)
+                    low = (total[n] - high.astype(jnp.float32)).astype(jnp.bfloat16)
+                    sums[which][r, n, pl.ds(k * strip, strip), :] = high
+                    sums[which][r, n, pl.ds(BS + k * strip, strip), :] = low
             return carry
 
-        lax.fori_loop(0, 2 * SLOTS, step, 0)
+        lax.fori_loop(0, 2, step, 0)
 
     def products(which):
-        unroll = 4
-
-        def step(i, carry):
-            for j in range(unroll):
-                o = i * unroll + j
-                q = cols_ref[8 * layer + o // SLOTS, lax.rem(o, SLOTS)]
-                four = jnp.dot(b_parts[which][o], p_split[which][q], preferred_element_type=jnp.float32)
+        pick_copy(which).wait()
+
+        def step(r, carry):
+            at = 8 * layer + r
+            for o in range(SLOTS):
+                q = cols_ref[o, at]
+                left = jnp.concatenate([sums[which][r, picks_smem[which][p, o, at]] for p in range(SLOTS)], axis=1)
+                four = jnp.dot(left, p_split[which][q], preferred_element_type=jnp.float32)
                 value = (four[BS:, BS:] + four[:BS, BS:] + four[BS:, :BS]) + four[:BS, :BS]
-                out_ref[o] = value if which == 1 else out_ref[o] + value
+                where = r * SLOTS + o
+                out_ref[where] = value if which == 1 else out_ref[where] + value
             return carry
 
-        lax.fori_loop(0, 8 * SLOTS // unroll, step, 0)
+        lax.fori_loop(0, 8, step, 0)
 
     events = []
     started = []
@@ -296,6 +308,9 @@
 
         codes_copy.start()
         p_local.start()
+        for which in range(2):
+            sums[which][:, 0] = jnp.zeros((8, 2 * BS, BS), jnp.bfloat16)
+        pick(0)
 
     def own_convert():
         p_local.wait()
@@ -303,6 +318,7 @@
 
     def codes_arrive():
         codes_copy.wait()
+        pick(1)
 
     add(0.0, start)
     add(2.0, own_convert)
@@ -453,10 +469,14 @@
             vmem((16, DEPTH, 2 * BS), bf16),
             vmem((8, DEPTH, BS), f32),
             vmem((8, DEPTH, BS), f32),
-            vmem((8 * SLOTS, 2 * BS, DEPTH), bf16),
-            vmem((8 * SLOTS, 2 * BS, DEPTH), bf16),
-            vmem((16, 8, BS), jnp.int32),
-            vmem((8, 8, BS), jnp.int32),
+            vmem((8, 16, 2 * BS, BS), bf16),
+            vmem((8, 16, 2 * BS, BS), bf16),
+            vmem((MP, 8, BS), jnp.int32),
+            vmem((MP, 8, BS), jnp.int32),
+            vmem((SLOTS, 8, BS), jnp.int32),
+            vmem((SLOTS, 8, BS), jnp.int32),
+            smem((SLOTS, 8, BS), jnp.int32),
+            smem((SLOTS, 8, BS), jnp.int32),
             dma((2, 4, 8)),
             dma((2, 4, 8)),
             dma((2, 2, 4)),
@@ -465,17 +485,17 @@
             dma((2, 4)),
             dma((2,)),
             dma((2,)),
-            dma((2,)),
+            dma((4,)),
         ],
         compiler_params=pltpu.CompilerParams(
-            collective_id=0, has_side_effects=True, vmem_limit_bytes=56 * 2**20
+            collective_id=0, has_side_effects=True, vmem_limit_bytes=44 * 2**20
         ),
         cost_estimate=pl.CostEstimate(flops=4 * 10**9, bytes_accessed=5 * 2**20, transcendentals=0),
     )(
         a_blocks.reshape(DEPTH, BS),
         p_blocks.reshape(DEPTH, BS),
-        out_columns,
-        pair_codes,
+        out_columns.T,
+        pair_codes.transpose(2, 1, 0),
     )
     return product.reshape(8, SLOTS, BS, BS)
 

time: 91.4 us -> 83.5 us (0.914)
  the two profiles are of different devices: /device:TPU:6 before, /device:TPU:2 now
where the time goes in v2:
time: 83.5 us; the launch traced here: 83.3 us
  Pallas kernels  78.6 us (94%)
  local copies, waits for them, and re-layouts  4.61 us (6%)
    pallas_call x1, Pallas kernels, shards(): pl.pallas_call(kernel, out_shape=jax.ShapeDtypeStruct((8 * SLOTS, BS, BS)...  78.6 us
    unnamed x9, local copies, waits for them, and re-layouts  4.61 us

profile of v2, /device:TPU:2, one launch (start us, length us, event | category | flops | bytes accessed | tf_op | source)
XLA Modules:
  0.0 83.3 jit_solution(11756428078018054442)
XLA Ops:
  0.0 0.0 copy-start
  0.0 0.9 %copy-done = f32[1,4,128,128]{3,2,1,0:T(8,128)S(1)} copy-done((f32[1,4,128,128]{3,2,1,0:T(8,128)S(1)}, f32[1,4,128,128]{3,2,1,0:T(8,128)}, u32[]{:S(2)}) %copy-start) | copy-done | bytes 262168
  1.0 0.0 copy-start.1
  1.0 0.9 %copy-done.1 = f32[1,4,128,128]{3,2,1,0:T(8,128)S(1)} copy-done((f32[1,4,128,128]{3,2,1,0:T(8,128)S(1)}, f32[1,4,128,128]{3,2,1,0:T(8,128)}, u32[]{:S(2)}) %copy-start.1) | copy-done | bytes 262168
  1.9 0.0 copy-start.2
  1.9 0.7 copy-done.2
  2.6 0.0 copy-start.3
  2.6 0.7 copy-done.3
  3.3 78.6 %shard_map.46 = f32[32,128,128]{2,1,0:T(8,128)S(1)} custom-call(f32[512,128]{1,0:T(8,128)S(1)} %bitcast.6, f32[512,128]{1,0:T(8,128)S(1)} %bitcast.7, s32[4,16]{1,0:T(4,128)S(1)} %bitcast.9, s32[7,4,16]{2,1,0:T(4,128)S(1)} %bitcast.8), custom_call_target="tpu_custom_call" | custom-call | flops 4000000000 | bytes 5242880 | tf_op jit(solution)/shard_map/pallas_call | solution.py:455
  81.9 1.3 %copy.6 = f32[8,4,128,128]{3,2,1,0:T(8,128)} copy(f32[8,4,128,128]{3,2,1,0:T(8,128)S(1)} %bitcast.5) | data formatting | bytes 4194304
Async XLA Ops:
  0.0 0.9 %copy-start = (f32[1,4,128,128]{3,2,1,0:T(8,128)S(1)}, f32[1,4,128,128]{3,2,1,0:T(8,128)}, u32[]{:S(2)}) copy-start(f32[1,4,128,128]{3,2,1,0:T(8,128)} %param.4) | copy-start | bytes 786436
  1.0 0.9 %copy-start.1 = (f32[1,4,128,128]{3,2,1,0:T(8,128)S(1)}, f32[1,4,128,128]{3,2,1,0:T(8,128)}, u32[]{:S(2)}) copy-start(f32[1,4,128,128]{3,2,1,0:T(8,128)} %param.5) | copy-start | bytes 786436
  1.9 0.7 copy-start.2
  2.6 0.7 copy-start.3

commit v3 on v2

v3 whole, which is shorter than its diff:
```python
import jax
import jax.numpy as jnp
from jax import lax
from jax.experimental import pallas as pl
from jax.experimental.pallas import tpu as pltpu
from jax.sharding import PartitionSpec as P

MESH = pl.DeviceIdType.MESH
BS = 128
SLOTS = 4
DEPTH = SLOTS * BS
MP = 7
NX, NY, NZ = 4, 8, 8
R1 = 224
GROUP = {1: (0, R1), 2: (R1, DEPTH - R1)}
ORDER = (
    ("P", 1, 0, -1), ("P", 1, 0, 1), ("P", 2, 0, -1), ("P", 1, -1, 0), ("P", 2, 0, 1), ("P", 1, 1, 0), ("P", 2, 1, 0),
    ("P", 2, -1, 0), ("P", 2, 0, 2), ("P", 2, 1, 1), ("P", 1, 0, 2), ("P", 2, -1, 1), ("P", 1, 1, 1), ("P", 2, 0, -2),
    ("P", 1, 0, -2), ("P", 2, -1, -1), ("P", 1, -1, -1), ("P", 1, -1, 1), ("P", 2, 2, 0), ("P", 1, 1, -1),
    ("P", 1, 2, 0), ("P", 2, 1, -1), ("M", 0), ("P", 2, -1, 2), ("P", 2, 0, 3), ("P", 2, 2, 1), ("P", 2, 1, 2),
    ("M", 1), ("H", 1, 1, 0), ("P", 1, 1, 2), ("H", 1, -1, 0), ("H", 1, -1, 1), ("P", 2, 1, -2), ("P", 2, -1, -2),
    ("H", 1, 1, 1), ("P", 1, 0, 3), ("C", 0, 1), ("P", 2, 2, -1), ("P", 2, 0, -3), ("P", 1, -1, 2), ("P", 1, 1, -2),
    ("P", 1, 2, 1), ("P", 1, -1, -2), ("P", 1, 2, -1), ("H", 2, 1, 0), ("C", 1, -1), ("P", 1, 0, -3), ("P", 2, 1, 3),
    ("C", 1, 1), ("P", 2, -1, 3), ("P", 2, 2, 2), ("H", 2, 1, 1), ("P", 2, 0, 4), ("H", 2, -1, 0), ("H", 2, -1, 1),
    ("H", 3, 1, 0), ("P", 1, 1, 3), ("C", 2, 1), ("C", 2, -1), ("H", 3, -1, 0), ("P", 2, -1, -3), ("P", 2, 1, -3),
    ("H", 3, 1, 1), ("P", 2, 2, -2), ("P", 1, 1, -3), ("P", 1, 0, 4), ("P", 1, -1, 3), ("H", 3, -1, 1),
    ("H", 4, 1, 0), ("P", 1, 2, 2), ("P", 1, 2, -2), ("C", 3, 1), ("P", 1, -1, -3), ("C", 3, -1), ("H", 4, 1, 1),
    ("P", 1, 1, 4), ("P", 2, 2, 3), ("P", 2, -1, 4), ("C", 4, 1), ("P", 2, 1, 4), ("P", 2, 2, -3), ("P", 1, -1, 4),
    ("P", 1, 2, 3), ("P", 2, 2, 4), ("P", 1, 2, -3), ("P", 1, 2, 4),
)


def onward(g, a, b):
    out = []
    if g == 1:
        if b == 0:
            if a == 0:
                out += [(1, 0, "x", 1), (-1, 0, "x", -1)]
            if a == 1:
                out += [(2, 0, "x", 1)]
            out += [(a, 1, "y", 1), (a, -1, "y", -1)]
        elif 0 < b < 4:
            out += [(a, b + 1, "y", 1)]
        elif -3 < b < 0:
            out += [(a, b - 1, "y", -1)]
    else:
        if a == 0:
            if b == 0:
                out += [(0, 1, "y", 1), (0, -1, "y", -1)]
            elif 0 < b < 4:
                out += [(0, b + 1, "y", 1)]
            elif -3 < b < 0:
                out += [(0, b - 1, "y", -1)]
            out += [(1, b, "x", 1), (-1, b, "x", -1)]
        elif a == 1:
            out += [(2, b, "x", 1)]
    return out


def kernel(
    a_ref, p_ref, cols_ref, codes_ref, out_ref,
    p_own, p_opp, ps_own, ps_opp, a_all, sums, cols, codes_in, codes_own, codes_opp,
    picks_own, picks_opp, picks_smem_own, picks_smem_opp,
    p_recv, p_send, a_recv, a_send, sib_recv, sib_send, move_send, codes_sem, local_sem,
):
    row, col, layer = lax.axis_index("row"), lax.axis_index("col"), lax.axis_index("layer")
    y, z, core = lax.rem(row, NY), col // 2, lax.rem(col, 2)
    x = (row // NY) * 2 + layer
    turn = 1 - 2 * core
    t = lax.rem(z + 2 * NZ - 4 * layer, NZ)
    q_me = row

    def device(x_, y_, z_, core_):
        return ((x_ // 2) * NY + y_, z_ * 2 + core_, lax.rem(x_, 2))

    def along(axis, way):
        if axis == "x":
            return device(lax.rem(x + NX + turn * way, NX), y, z, core)
        if axis == "y":
            return device(x, lax.rem(y + NY + turn * way, NY), z, core)
        return device(x, y, lax.rem(z + NZ + turn * way, NZ), core)

    sibling = device(x, y, z, 1 - core)
    partner = (row, col, 1 - layer)
    mover = (row, (NZ - 1 - z) * 2 + core, 1 - layer)

    codes_load = pltpu.make_async_copy(codes_ref, codes_in, local_sem.at[4])
    cols_load = pltpu.make_async_copy(cols_ref, cols, local_sem.at[5])
    codes_load.start()
    cols_load.start()

    barrier = pltpu.get_barrier_semaphore()
    greeted = [along(axis, way) for axis in "xyz" for way in (1, -1)] + [sibling, mover]
    for other in greeted:
        pl.semaphore_signal(barrier, inc=1, device_id=other, device_id_type=MESH)
    pl.semaphore_wait(barrier, len(greeted))

    p_land = (p_own, p_opp)
    p_split = (ps_own, ps_opp)
    picks = (picks_own, picks_opp)
    picks_smem = (picks_smem_own, picks_smem_opp)
    codes_land = (codes_own, codes_opp)

    def p_slot(a, b):
        x0 = lax.rem(x + 2 * NX - turn * a, NX)
        y0 = lax.rem(y + 2 * NY - turn * b, NY)
        return (x0 // 2) * NY + y0


    def p_piece(g, a, b):
        lo, size = GROUP[g]
        return p_land[a % 2].at[p_slot(a, b), pl.ds(lo, size)]

    def p_forward(g, a, b):
        lo, size = GROUP[g]
        src = p_ref.at[pl.ds(lo, size)] if (a, b) == (0, 0) else p_piece(g, a, b)
        copies = []
        for a2, b2, axis, way in onward(g, a, b):
            copies.append(
                pltpu.make_async_remote_copy(
                    src_ref=src,
                    dst_ref=p_land[a2 % 2].at[p_slot(a, b), pl.ds(lo, size)],
                    send_sem=p_send.at[g - 1, a2 + 1, b2 + 3],
                    recv_sem=p_recv.at[g - 1, a2 + 1, b2 + 3],
                    device_id=along(axis, way),
                    device_id_type=MESH,
                )
            )
        return copies

    def p_wait(g, a, b):
        here = p_piece(g, a, b)
        pltpu.make_async_remote_copy(
            src_ref=here,
            dst_ref=here,
            send_sem=p_send.at[g - 1, a + 1, b + 3],
            recv_sem=p_recv.at[g - 1, a + 1, b + 3],
            device_id=along("x", 1),
            device_id_type=MESH,
        ).wait_recv()

    def p_convert(a, b, lo, size):
        q = p_slot(a, b)
        value = p_land[a % 2][q, pl.ds(lo, size), :]
        high = value.astype(jnp.bfloat16)
        low = (value - high.astype(jnp.float32)).astype(jnp.bfloat16)
        p_split[a % 2][q, pl.ds(lo, size), pl.ds(0, BS)] = high
        p_split[a % 2][q, pl.ds(lo, size), pl.ds(BS, BS)] = low

    half = DEPTH // 2

    def rows_of(e):
        return jnp.where(e < 4, 2 * e, 8 + 2 * (7 - e))

    def a_half(e, h):
        return a_all.at[rows_of(e) + core, pl.ds(h * half, half)]

    def a_copy(e, h, d, way, src=None):
        return pltpu.make_async_remote_copy(
            src_ref=a_half(e, h) if src is None else src,
            dst_ref=a_half(e, h),
            send_sem=a_send.at[h, (1 - way) // 2, d],
            recv_sem=a_recv.at[h, e],
            device_id=along("z", way),
            device_id_type=MESH,
        )

    def a_wait(e, h):
        a_copy(e, h, 0, 1).wait_recv()

    def sib_copy(e, src=None):
        here = a_all.at[rows_of(e) + core]
        return pltpu.make_async_remote_copy(
            src_ref=here if src is None else src,
            dst_ref=here,
            send_sem=sib_send.at[e],
            recv_sem=sib_recv.at[e],
            device_id=sibling,
            device_id_type=MESH,
        )

    def sib_wait(e):
        there = a_all.at[rows_of(e) + 1 - core]
        pltpu.make_async_remote_copy(
            src_ref=there,
            dst_ref=there,
            send_sem=sib_send.at[e],
            recv_sem=sib_recv.at[e],
            device_id=sibling,
            device_id_type=MESH,
        ).wait_recv()

    def move_copy(h):
        return pltpu.make_async_remote_copy(
            src_ref=a_ref.at[pl.ds(h * half, half)],
            dst_ref=a_half(11 - t, h),
            send_sem=move_send.at[h],
            recv_sem=a_recv.at[h, 11 - t],
            device_id=mover,
            device_id_type=MESH,
        )

    def source(d, way):
        return lax.rem(t + 2 * NZ - turn * way * d, NZ)

    def goes_on(d, way):
        return d < (4 if way == 1 else 3)

    codes_copy = pltpu.make_async_remote_copy(
        src_ref=codes_own,
        dst_ref=codes_opp,
        send_sem=codes_sem.at[0],
        recv_sem=codes_sem.at[1],
        device_id=partner,
        device_id_type=MESH,
    )

    def pick_copy(which):
        return pltpu.make_async_copy(picks[which], picks_smem[which], local_sem.at[2 + which])

    def pick(which):
        codes = [codes_land[which][m] for m in range(MP)]
        for p in range(SLOTS):
            total = jnp.zeros((8, BS), jnp.int32)
            for code in codes:
                for a in range(SLOTS):
                    total += jnp.where(code == a * SLOTS + p, 1 << a, 0)
            picks[which][p] = total
        pick_copy(which).start()

    def combine(e):
        def step(i, carry):
            r = rows_of(e) + i
            strip = 16
            for k in range(BS // strip):
                total = {0: None}
                for n in range(1, 16):
                    a = n.bit_length() - 1
                    part = a_all[r, pl.ds(a * BS + k * strip, strip), :] if n == 1 << a else None
                    total[n] = part if n == 1 << a else total[n - (1 << a)] + total[1 << a]
                    high = total[n].astype(jnp.bfloat16)
                    low = (total[n] - high.astype(jnp.float32)).astype(jnp.bfloat16)
                    sums[r, n, pl.ds(k * strip, strip), :] = high
                    sums[r, n, pl.ds(BS + k * strip, strip), :] = low
            return carry

        lax.fori_loop(0, 2, step, 0)

    def products(which):
        pick_copy(which).wait()

        def step(r, carry):
            at = 8 * layer + r
            for o in range(SLOTS):
                q = cols[o, at]
                left = jnp.concatenate([sums[8 * which + r, picks_smem[which][p, o, at]] for p in range(SLOTS)], axis=1)
                four = jnp.dot(left, p_split[which][q], preferred_element_type=jnp.float32)
                value = (four[BS:, BS:] + four[:BS, BS:] + four[BS:, :BS]) + four[:BS, :BS]
                where = r * SLOTS + o
                out_ref[where] = value if which == 1 else out_ref[where] + value
            return carry

        lax.fori_loop(0, 8, step, 0)

    p_local = pltpu.make_async_copy(p_ref, p_own.at[q_me], local_sem.at[0])
    a_local = pltpu.make_async_copy(a_ref, a_all.at[rows_of(lax.rem(t, 4)) + core], local_sem.at[1])

    @pl.when(t >= 4)
    def _():
        for h in range(2):
            move_copy(h).start()

    for copy in p_forward(2, 0, 0) + p_forward(1, 0, 0):
        copy.start()

    @pl.when(t < 4)
    def _():
        for h in range(2):
            for way in (1, -1):
                a_copy(t, h, 0, way, a_ref.at[pl.ds(h * half, half)]).start()
        a_local.start()
        sib_copy(t, a_ref).start()

    p_local.start()
    codes_own[...] = jnp.full(codes_own.shape, SLOTS * SLOTS, jnp.int32)
    codes_load.wait()
    codes_own[:, pl.ds(0, SLOTS), pl.ds(0, 16)] = codes_in[...]
    codes_copy.start()
    cols_load.wait()
    pick(0)
    sums[:, 0] = jnp.zeros((16, 2 * BS, BS), jnp.bfloat16)
    p_local.wait()
    p_convert(0, 0, 0, DEPTH)
    codes_copy.wait()
    pick(1)

    def piece_of_p(g, a, b):
        p_wait(g, a, b)
        for copy in p_forward(g, a, b):
            copy.start()
        p_convert(a, b, *GROUP[g])

    def moved(h):
        @pl.when(t >= 4)
        def _():
            a_wait(t, h)
            for way in (1, -1):
                a_copy(t, h, 0, way).start()
            if h == 1:
                sib_copy(t).start()

    def hop(d, way, h):
        e = source(d, way)
        a_wait(e, h)
        if goes_on(d, way):
            a_copy(e, h, d, way).start()
        if h == 1:
            sib_copy(e).start()

    def add_up(d, way):
        if d == 0:

            @pl.when(t < 4)
            def _():
                a_local.wait()

        e = source(d, way)
        sib_wait(e)
        combine(e)

    steps = {"P": piece_of_p, "M": moved, "H": hop, "C": add_up}
    for name, *where in ORDER:
        steps[name](*where)
    products(1)
    products(0)

    for g in (1, 2):
        for a in range(-1, 3):
            for b in range(-3, 5):
                for copy in p_forward(g, a, b):
                    copy.wait_send()

    @pl.when(t >= 4)
    def _():
        for h in range(2):
            move_copy(h).wait_send()

    for d in range(5):
        for way in (1, -1):
            if (d == 4 and way == -1) or (d == 0 and way == -1):
                continue
            e = source(d, way)
            sib_copy(e).wait_send()
    for d in range(4):
        for way in (1, -1):
            if goes_on(d, way):
                for h in range(2):
                    a_copy(source(d, way), h, d, way).wait_send()


def shards(a_blocks, p_blocks, out_columns, pair_codes):
    vmem, smem = pltpu.VMEM, pltpu.SMEM
    dma = pltpu.SemaphoreType.DMA
    f32, bf16 = jnp.float32, jnp.bfloat16
    operands = (
        a_blocks.reshape(DEPTH, BS),
        p_blocks.reshape(DEPTH, BS),
        out_columns.T,
        pair_codes.transpose(2, 1, 0),
    )
    product = pl.pallas_call(
        kernel,
        out_shape=jax.ShapeDtypeStruct((8 * SLOTS, BS, BS), f32),
        in_specs=[
            pl.BlockSpec(memory_space=pltpu.HBM),
            pl.BlockSpec(memory_space=pltpu.HBM),
            pl.BlockSpec(memory_space=pltpu.HBM),
            pl.BlockSpec(memory_space=pltpu.HBM),
        ],
        out_specs=pl.BlockSpec(memory_space=vmem),
        scratch_shapes=[
            vmem((16, DEPTH, BS), f32),
            vmem((16, DEPTH, BS), f32),
            vmem((16, DEPTH, 2 * BS), bf16),
            vmem((16, DEPTH, 2 * BS), bf16),
            vmem((16, DEPTH, BS), f32),
            vmem((16, 16, 2 * BS, BS), bf16),
            smem((SLOTS, 16), jnp.int32),
            vmem((MP, SLOTS, 16), jnp.int32),
            vmem((MP, 8, BS), jnp.int32),
            vmem((MP, 8, BS), jnp.int32),
            vmem((SLOTS, 8, BS), jnp.int32),
            vmem((SLOTS, 8, BS), jnp.int32),
            smem((SLOTS, 8, BS), jnp.int32),
            smem((SLOTS, 8, BS), jnp.int32),
            dma((2, 4, 8)),
            dma((2, 4, 8)),
            dma((2, 8)),
            dma((2, 2, 4)),
            dma((8,)),
            dma((8,)),
            dma((2,)),
            dma((2,)),
            dma((6,)),
        ],
        compiler_params=pltpu.CompilerParams(
            collective_id=0, has_side_effects=True, vmem_limit_bytes=44 * 2**20
        ),
        cost_estimate=pl.CostEstimate(flops=4 * 10**9, bytes_accessed=5 * 2**20, transcendentals=0),
    )(*(pltpu.with_memory_space_constraint(operand, pltpu.HBM) for operand in operands))
    return product.reshape(8, SLOTS, BS, BS)


def solution(mesh):
    return jax.shard_map(
        shards,
        mesh=mesh,
        in_specs=(
            P(("row", "col"), "layer", None, None),
            P(("row", "col"), "layer", None, None),
            P("row", "col"),
            P("row", "col", "layer"),
        ),
        out_specs=P(("row", "layer"), "col", None, None),
        check_vma=False,
    )
```

time: 83.5 us -> 81.7 us (0.978)
  the two profiles are of different devices: /device:TPU:2 before, /device:TPU:6 now
where the time goes in v3:
time: 81.7 us; the launch traced here: 81.5 us
  Pallas kernels  80.2 us (98%)
  local copies, waits for them, and re-layouts  1.32 us (2%)
    pallas_call x1, Pallas kernels, shards(): pl.pallas_call(kernel, out_shape=jax.ShapeDtypeStruct((8 * SLOTS, BS, BS)...  80.2 us

profile of v3, /device:TPU:6, one launch (start us, length us, event | category | flops | bytes accessed | tf_op | source)
XLA Modules:
  0.0 81.5 jit_solution(10801879613889526151)
XLA Ops:
  0.0 80.2 %shard_map.46 = f32[32,128,128]{2,1,0:T(8,128)S(1)} custom-call(f32[512,128]{1,0:T(8,128)} %bitcast.6, f32[512,128]{1,0:T(8,128)} %bitcast.7, s32[4,16]{1,0:T(4,128)} %bitcast.9, s32[7,4,16]{2,1,0:T(4,128)} %bitcast.8), custom_call_target="tpu_custom_call" | custom-call | flops 4000000000 | bytes 5242880 | tf_op jit(solution)/shard_map/pallas_call | solution.py:371
  80.2 1.3 %copy.6 = f32[8,4,128,128]{3,2,1,0:T(8,128)} copy(f32[8,4,128,128]{3,2,1,0:T(8,128)S(1)} %bitcast.5) | data formatting | bytes 4194304

commit v4 on v3

--- a/solution.py
+++ b/solution.py
@@ -14,20 +14,22 @@
 R1 = 224
 GROUP = {1: (0, R1), 2: (R1, DEPTH - R1)}
 ORDER = (
-    ("P", 1, 0, -1), ("P", 1, 0, 1), ("P", 2, 0, -1), ("P", 1, -1, 0), ("P", 2, 0, 1), ("P", 1, 1, 0), ("P", 2, 1, 0),
-    ("P", 2, -1, 0), ("P", 2, 0, 2), ("P", 2, 1, 1), ("P", 1, 0, 2), ("P", 2, -1, 1), ("P", 1, 1, 1), ("P", 2, 0, -2),
-    ("P", 1, 0, -2), ("P", 2, -1, -1), ("P", 1, -1, -1), ("P", 1, -1, 1), ("P", 2, 2, 0), ("P", 1, 1, -1),
-    ("P", 1, 2, 0), ("P", 2, 1, -1), ("M", 0), ("P", 2, -1, 2), ("P", 2, 0, 3), ("P", 2, 2, 1), ("P", 2, 1, 2),
-    ("M", 1), ("H", 1, 1, 0), ("P", 1, 1, 2), ("H", 1, -1, 0), ("H", 1, -1, 1), ("P", 2, 1, -2), ("P", 2, -1, -2),
-    ("H", 1, 1, 1), ("P", 1, 0, 3), ("C", 0, 1), ("P", 2, 2, -1), ("P", 2, 0, -3), ("P", 1, -1, 2), ("P", 1, 1, -2),
-    ("P", 1, 2, 1), ("P", 1, -1, -2), ("P", 1, 2, -1), ("H", 2, 1, 0), ("C", 1, -1), ("P", 1, 0, -3), ("P", 2, 1, 3),
-    ("C", 1, 1), ("P", 2, -1, 3), ("P", 2, 2, 2), ("H", 2, 1, 1), ("P", 2, 0, 4), ("H", 2, -1, 0), ("H", 2, -1, 1),
-    ("H", 3, 1, 0), ("P", 1, 1, 3), ("C", 2, 1), ("C", 2, -1), ("H", 3, -1, 0), ("P", 2, -1, -3), ("P", 2, 1, -3),
-    ("H", 3, 1, 1), ("P", 2, 2, -2), ("P", 1, 1, -3), ("P", 1, 0, 4), ("P", 1, -1, 3), ("H", 3, -1, 1),
-    ("H", 4, 1, 0), ("P", 1, 2, 2), ("P", 1, 2, -2), ("C", 3, 1), ("P", 1, -1, -3), ("C", 3, -1), ("H", 4, 1, 1),
-    ("P", 1, 1, 4), ("P", 2, 2, 3), ("P", 2, -1, 4), ("C", 4, 1), ("P", 2, 1, 4), ("P", 2, 2, -3), ("P", 1, -1, 4),
-    ("P", 1, 2, 3), ("P", 2, 2, 4), ("P", 1, 2, -3), ("P", 1, 2, 4),
+    ("P", 1, 0, -1), ("X", 0), ("P", 1, -1, 0), ("P", 2, 0, 1), ("X", 1), ("P", 1, 0, 1), ("P", 2, 0, -1), ("X", -1),
+    ("P", 2, 0, 2), ("X", 2), ("P", 1, 1, 0), ("P", 2, 0, -2), ("P", 2, -1, 0), ("P", 2, 1, 0), ("P", 1, 0, 2),
+    ("P", 1, -1, -1), ("P", 2, -1, -1), ("P", 1, 0, -2), ("P", 1, -1, 1), ("X", -2), ("M", 0), ("P", 2, -1, 1),
+    ("P", 1, 2, 0), ("P", 1, 1, -1), ("P", 1, 1, 1), ("P", 2, 1, 1), ("P", 2, 0, 3), ("X", 3), ("P", 2, 1, -1),
+    ("M", 1), ("P", 2, -1, 2), ("H", 1, 1, 0), ("C", 0, 1), ("H", 1, -1, 0), ("P", 2, 1, -2), ("P", 2, 1, 2),
+    ("P", 2, 2, 0), ("H", 1, 1, 1), ("P", 1, 1, 2), ("P", 2, -1, -2), ("P", 1, 0, 3), ("H", 1, -1, 1), ("P", 2, 2, 1),
+    ("C", 1, -1), ("P", 2, 0, -3), ("P", 1, -1, 2), ("X", -3), ("H", 2, 1, 0), ("C", 1, 1), ("H", 2, 1, 1),
+    ("P", 1, 1, -2), ("H", 2, -1, 0), ("P", 1, -1, -2), ("P", 2, 2, -1), ("P", 2, -1, 3), ("P", 1, 2, -1),
+    ("P", 1, 0, -3), ("P", 1, 2, 1), ("P", 2, 0, 4), ("X", 4), ("P", 1, 0, 4), ("H", 2, -1, 1), ("C", 2, 1),
+    ("H", 3, 1, 0), ("C", 2, -1), ("H", 3, -1, 0), ("P", 1, 1, -3), ("P", 2, 2, 2), ("H", 3, 1, 1), ("P", 2, 1, 3),
+    ("P", 1, -1, 3), ("H", 3, -1, 1), ("P", 1, 1, 3), ("H", 4, 1, 0), ("P", 2, -1, -3), ("P", 2, 2, -2),
+    ("P", 2, 1, -3), ("C", 3, 1), ("P", 1, 2, 2), ("H", 4, 1, 1), ("P", 1, -1, -3), ("C", 3, -1), ("P", 2, 1, 4),
+    ("P", 1, 2, -2), ("P", 2, -1, 4), ("C", 4, 1), ("P", 1, -1, 4), ("P", 1, 1, 4), ("Q", 0), ("P", 1, 2, 3),
+    ("Q", 3), ("Q", 1), ("P", 2, 2, 3), ("Q", 2), ("P", 2, 2, -3), ("P", 1, 2, 4), ("P", 1, 2, -3), ("P", 2, 2, 4),
 )
+QUARTERS = 4
 
 
 def onward(g, a, b):
@@ -111,11 +113,13 @@
         lo, size = GROUP[g]
         return p_land[a % 2].at[p_slot(a, b), pl.ds(lo, size)]
 
-    def p_forward(g, a, b):
+    def p_forward(g, a, b, axes="xy"):
         lo, size = GROUP[g]
         src = p_ref.at[pl.ds(lo, size)] if (a, b) == (0, 0) else p_piece(g, a, b)
         copies = []
         for a2, b2, axis, way in onward(g, a, b):
+            if axis not in axes:
+                continue
             copies.append(
                 pltpu.make_async_remote_copy(
                     src_ref=src,
@@ -246,10 +250,9 @@
 
         lax.fori_loop(0, 2, step, 0)
 
-    def products(which):
-        pick_copy(which).wait()
-
-        def step(r, carry):
+    def products(which, first, count):
+        def step(i, carry):
+            r = first + i
             at = 8 * layer + r
             for o in range(SLOTS):
                 q = cols[o, at]
@@ -260,7 +263,7 @@
                 out_ref[where] = value if which == 1 else out_ref[where] + value
             return carry
 
-        lax.fori_loop(0, 8, step, 0)
+        lax.fori_loop(0, count, step, 0)
 
     p_local = pltpu.make_async_copy(p_ref, p_own.at[q_me], local_sem.at[0])
     a_local = pltpu.make_async_copy(a_ref, a_all.at[rows_of(lax.rem(t, 4)) + core], local_sem.at[1])
@@ -270,7 +273,7 @@
         for h in range(2):
             move_copy(h).start()
 
-    for copy in p_forward(2, 0, 0) + p_forward(1, 0, 0):
+    for copy in p_forward(1, 0, 0) + p_forward(2, 0, 0, "y"):
         copy.start()
 
     @pl.when(t < 4)
@@ -293,12 +296,18 @@
     p_convert(0, 0, 0, DEPTH)
     codes_copy.wait()
     pick(1)
+    for which in range(2):
+        pick_copy(which).wait()
 
     def piece_of_p(g, a, b):
         p_wait(g, a, b)
-        for copy in p_forward(g, a, b):
+        for copy in p_forward(g, a, b, "y" if (g, a) == (2, 0) else "xy"):
             copy.start()
         p_convert(a, b, *GROUP[g])
+
+    def across(b):
+        for copy in p_forward(2, 0, b, "x"):
+            copy.start()
 
     def moved(h):
         @pl.when(t >= 4)
@@ -328,11 +337,13 @@
         sib_wait(e)
         combine(e)
 
-    steps = {"P": piece_of_p, "M": moved, "H": hop, "C": add_up}
+    def quarter(i):
+        products(1, i * 8 // QUARTERS, 8 // QUARTERS)
+
+    steps = {"P": piece_of_p, "M": moved, "H": hop, "C": add_up, "X": across, "Q": quarter}
     for name, *where in ORDER:
         steps[name](*where)
-    products(1)
-    products(0)
+    products(0, 0, 8)
 
     for g in (1, 2):
         for a in range(-1, 3):

time: 81.7 us -> 76.7 us (0.939)
  Pallas kernels: 80.2 us -> 75.2 us
    pallas_call x1, Pallas kernels: 80.2 us -> 75.2 us  [shards(): pl.pallas_call(kernel, out_shape=jax.ShapeDtypeStruct((8 * SLOTS, BS, BS)...]
where the time goes in v4:
time: 76.7 us; the launch traced here: 76.6 us
  Pallas kernels  75.2 us (98%)
  local copies, waits for them, and re-layouts  1.32 us (2%)
    pallas_call x1, Pallas kernels, shards(): pl.pallas_call(kernel, out_shape=jax.ShapeDtypeStruct((8 * SLOTS, BS, BS)...  75.2 us

profile of v4, /device:TPU:6, one launch (start us, length us, event | category | flops | bytes accessed | tf_op | source)
XLA Modules:
  0.0 76.6 jit_solution(15571610004058111525)
XLA Ops:
  0.0 75.2 %shard_map.46 = f32[32,128,128]{2,1,0:T(8,128)S(1)} custom-call(f32[512,128]{1,0:T(8,128)} %bitcast.6, f32[512,128]{1,0:T(8,128)} %bitcast.7, s32[4,16]{1,0:T(4,128)} %bitcast.9, s32[7,4,16]{2,1,0:T(4,128)} %bitcast.8), custom_call_target="tpu_custom_call" | custom-call | flops 4000000000 | bytes 5242880 | tf_op jit(solution)/shard_map/pallas_call | solution.py:382
  75.3 1.3 %copy.6 = f32[8,4,128,128]{3,2,1,0:T(8,128)} copy(f32[8,4,128,128]{3,2,1,0:T(8,128)S(1)} %bitcast.5) | data formatting | bytes 4194304

commit v5 on v4

--- a/solution.py
+++ b/solution.py
@@ -11,23 +11,23 @@
 DEPTH = SLOTS * BS
 MP = 7
 NX, NY, NZ = 4, 8, 8
-R1 = 224
+R1 = 208
 GROUP = {1: (0, R1), 2: (R1, DEPTH - R1)}
 ORDER = (
-    ("P", 1, 0, -1), ("X", 0), ("P", 1, -1, 0), ("P", 2, 0, 1), ("X", 1), ("P", 1, 0, 1), ("P", 2, 0, -1), ("X", -1),
-    ("P", 2, 0, 2), ("X", 2), ("P", 1, 1, 0), ("P", 2, 0, -2), ("P", 2, -1, 0), ("P", 2, 1, 0), ("P", 1, 0, 2),
-    ("P", 1, -1, -1), ("P", 2, -1, -1), ("P", 1, 0, -2), ("P", 1, -1, 1), ("X", -2), ("M", 0), ("P", 2, -1, 1),
-    ("P", 1, 2, 0), ("P", 1, 1, -1), ("P", 1, 1, 1), ("P", 2, 1, 1), ("P", 2, 0, 3), ("X", 3), ("P", 2, 1, -1),
-    ("M", 1), ("P", 2, -1, 2), ("H", 1, 1, 0), ("C", 0, 1), ("H", 1, -1, 0), ("P", 2, 1, -2), ("P", 2, 1, 2),
-    ("P", 2, 2, 0), ("H", 1, 1, 1), ("P", 1, 1, 2), ("P", 2, -1, -2), ("P", 1, 0, 3), ("H", 1, -1, 1), ("P", 2, 2, 1),
-    ("C", 1, -1), ("P", 2, 0, -3), ("P", 1, -1, 2), ("X", -3), ("H", 2, 1, 0), ("C", 1, 1), ("H", 2, 1, 1),
-    ("P", 1, 1, -2), ("H", 2, -1, 0), ("P", 1, -1, -2), ("P", 2, 2, -1), ("P", 2, -1, 3), ("P", 1, 2, -1),
-    ("P", 1, 0, -3), ("P", 1, 2, 1), ("P", 2, 0, 4), ("X", 4), ("P", 1, 0, 4), ("H", 2, -1, 1), ("C", 2, 1),
-    ("H", 3, 1, 0), ("C", 2, -1), ("H", 3, -1, 0), ("P", 1, 1, -3), ("P", 2, 2, 2), ("H", 3, 1, 1), ("P", 2, 1, 3),
-    ("P", 1, -1, 3), ("H", 3, -1, 1), ("P", 1, 1, 3), ("H", 4, 1, 0), ("P", 2, -1, -3), ("P", 2, 2, -2),
-    ("P", 2, 1, -3), ("C", 3, 1), ("P", 1, 2, 2), ("H", 4, 1, 1), ("P", 1, -1, -3), ("C", 3, -1), ("P", 2, 1, 4),
-    ("P", 1, 2, -2), ("P", 2, -1, 4), ("C", 4, 1), ("P", 1, -1, 4), ("P", 1, 1, 4), ("Q", 0), ("P", 1, 2, 3),
-    ("Q", 3), ("Q", 1), ("P", 2, 2, 3), ("Q", 2), ("P", 2, 2, -3), ("P", 1, 2, 4), ("P", 1, 2, -3), ("P", 2, 2, 4),
+    ("X", 0), ("P", 1, -1, 0), ("P", 2, 0, -1), ("P", 2, 0, 1), ("X", 1), ("P", 1, 0, -1), ("X", -1), ("N",),
+    ("P", 2, 0, 2), ("X", 2), ("P", 1, 1, 0), ("P", 2, -1, 0), ("P", 2, 0, -2), ("P", 1, 0, 1), ("M", 0), ("M", 1),
+    ("X", -2), ("P", 1, 1, 1), ("P", 2, 1, 0), ("P", 1, -1, 1), ("P", 2, -1, -1), ("P", 1, 0, -2), ("P", 1, 2, 0),
+    ("P", 1, 1, -1), ("P", 2, -1, 1), ("P", 2, 1, -1), ("P", 1, -1, -1), ("P", 1, 0, 2), ("P", 2, 1, 1),
+    ("H", 1, 1, 0), ("H", 1, -1, 0), ("P", 2, 0, 3), ("X", 3), ("H", 1, -1, 1), ("H", 1, 1, 1), ("P", 2, 1, -2),
+    ("C", 0, 1), ("H", 2, 1, 0), ("P", 1, 1, 2), ("H", 2, 1, 1), ("P", 2, 1, 2), ("P", 2, -1, 2), ("H", 2, -1, 0),
+    ("P", 1, 0, 3), ("P", 2, 0, -3), ("X", -3), ("P", 1, -1, 2), ("P", 1, 1, -2), ("P", 1, 2, -1), ("C", 1, 1),
+    ("P", 2, 2, 0), ("H", 3, 1, 0), ("P", 2, 0, 4), ("H", 2, -1, 1), ("P", 1, 2, 1), ("X", 4), ("C", 1, -1),
+    ("P", 1, -1, -2), ("C", 2, 1), ("H", 3, 1, 1), ("P", 2, -1, -2), ("P", 2, 2, 1), ("P", 1, 0, -3), ("P", 2, -1, 3),
+    ("H", 3, -1, 0), ("P", 1, 1, 3), ("C", 2, -1), ("H", 3, -1, 1), ("P", 1, -1, 3), ("P", 1, 1, -3), ("P", 2, 1, -3),
+    ("H", 4, 1, 0), ("P", 2, 2, 2), ("P", 2, 2, -1), ("C", 3, -1), ("P", 2, 2, -2), ("P", 1, 1, 4), ("H", 4, 1, 1),
+    ("C", 3, 1), ("P", 1, 2, 2), ("P", 2, -1, -3), ("P", 1, -1, 4), ("P", 1, 0, 4), ("P", 2, 1, 4), ("P", 2, 1, 3),
+    ("P", 1, -1, -3), ("P", 1, 2, -2), ("C", 4, 1), ("P", 2, -1, 4), ("Q", 0), ("Q", 1), ("P", 1, 2, 3), ("Q", 3),
+    ("P", 1, 2, -3), ("Q", 2), ("P", 2, 2, 4), ("P", 2, 2, -3), ("P", 1, 2, 4), ("P", 2, 2, 3),
 )
 QUARTERS = 4
 
@@ -63,7 +63,7 @@
     a_ref, p_ref, cols_ref, codes_ref, out_ref,
     p_own, p_opp, ps_own, ps_opp, a_all, sums, cols, codes_in, codes_own, codes_opp,
     picks_own, picks_opp, picks_smem_own, picks_smem_opp,
-    p_recv, p_send, a_recv, a_send, sib_recv, sib_send, move_send, codes_sem, local_sem,
+    passing, p_recv, p_send, a_recv, a_send, sib_recv, sib_send, move_send, pass_sem, codes_sem, local_sem,
 ):
     row, col, layer = lax.axis_index("row"), lax.axis_index("col"), lax.axis_index("layer")
     y, z, core = lax.rem(row, NY), col // 2, lax.rem(col, 2)
@@ -85,6 +85,7 @@
     sibling = device(x, y, z, 1 - core)
     partner = (row, col, 1 - layer)
     mover = (row, (NZ - 1 - z) * 2 + core, 1 - layer)
+    opposite = (row, (NZ - 1 - z) * 2 + core, layer)
 
     codes_load = pltpu.make_async_copy(codes_ref, codes_in, local_sem.at[4])
     cols_load = pltpu.make_async_copy(cols_ref, cols, local_sem.at[5])
@@ -92,7 +93,7 @@
     cols_load.start()
 
     barrier = pltpu.get_barrier_semaphore()
-    greeted = [along(axis, way) for axis in "xyz" for way in (1, -1)] + [sibling, mover]
+    greeted = [along(axis, way) for axis in "xyz" for way in (1, -1)] + [sibling, mover, opposite]
     for other in greeted:
         pl.semaphore_signal(barrier, inc=1, device_id=other, device_id_type=MESH)
     pl.semaphore_wait(barrier, len(greeted))
@@ -194,15 +195,30 @@
             device_id_type=MESH,
         ).wait_recv()
 
-    def move_copy(h):
-        return pltpu.make_async_remote_copy(
-            src_ref=a_ref.at[pl.ds(h * half, half)],
-            dst_ref=a_half(11 - t, h),
-            send_sem=move_send.at[h],
-            recv_sem=a_recv.at[h, 11 - t],
-            device_id=mover,
-            device_id_type=MESH,
-        )
+    move_copy = pltpu.make_async_remote_copy(
+        src_ref=a_ref.at[pl.ds(0, half)],
+        dst_ref=a_half(11 - t, 0),
+        send_sem=move_send.at[0],
+        recv_sem=a_recv.at[0, 11 - t],
+        device_id=mover,
+        device_id_type=MESH,
+    )
+    pass_copy = pltpu.make_async_remote_copy(
+        src_ref=a_ref.at[pl.ds(half, half)],
+        dst_ref=passing,
+        send_sem=pass_sem.at[0],
+        recv_sem=pass_sem.at[1],
+        device_id=opposite,
+        device_id_type=MESH,
+    )
+    cross_copy = pltpu.make_async_remote_copy(
+        src_ref=passing,
+        dst_ref=a_half(t + 4, 1),
+        send_sem=move_send.at[1],
+        recv_sem=a_recv.at[1, t + 4],
+        device_id=partner,
+        device_id_type=MESH,
+    )
 
     def source(d, way):
         return lax.rem(t + 2 * NZ - turn * way * d, NZ)
@@ -270,8 +286,8 @@
 
     @pl.when(t >= 4)
     def _():
-        for h in range(2):
-            move_copy(h).start()
+        move_copy.start()
+        pass_copy.start()
 
     for copy in p_forward(1, 0, 0) + p_forward(2, 0, 0, "y"):
         copy.start()
@@ -318,6 +334,12 @@
             if h == 1:
                 sib_copy(t).start()
 
+    def cross():
+        @pl.when(t < 4)
+        def _():
+            pass_copy.wait_recv()
+            cross_copy.start()
+
     def hop(d, way, h):
         e = source(d, way)
         a_wait(e, h)
@@ -340,7 +362,7 @@
     def quarter(i):
         products(1, i * 8 // QUARTERS, 8 // QUARTERS)
 
-    steps = {"P": piece_of_p, "M": moved, "H": hop, "C": add_up, "X": across, "Q": quarter}
+    steps = {"P": piece_of_p, "M": moved, "H": hop, "C": add_up, "N": cross, "X": across, "Q": quarter}
     for name, *where in ORDER:
         steps[name](*where)
     products(0, 0, 8)
@@ -353,8 +375,12 @@
 
     @pl.when(t >= 4)
     def _():
-        for h in range(2):
-            move_copy(h).wait_send()
+        move_copy.wait_send()
+        pass_copy.wait_send()
+
+    @pl.when(t < 4)
+    def _():
+        cross_copy.wait_send()
 
     for d in range(5):
         for way in (1, -1):
@@ -404,12 +430,14 @@
             vmem((SLOTS, 8, BS), jnp.int32),
             smem((SLOTS, 8, BS), jnp.int32),
             smem((SLOTS, 8, BS), jnp.int32),
+            vmem((DEPTH // 2, BS), f32),
             dma((2, 4, 8)),
             dma((2, 4, 8)),
             dma((2, 8)),
             dma((2, 2, 4)),
             dma((8,)),
             dma((8,)),
+            dma((2,)),
             dma((2,)),
             dma((2,)),
             dma((6,)),

time: 76.7 us -> 74.2 us (0.967)
  Pallas kernels: 75.2 us -> 72.7 us
    pallas_call x1, Pallas kernels: 75.2 us -> 72.7 us  [shards(): pl.pallas_call(kernel, out_shape=jax.ShapeDtypeStruct((8 * SLOTS, BS, BS)...]
where the time goes in v5:
time: 74.2 us; the launch traced here: 74.1 us
  Pallas kernels  72.7 us (98%)
  local copies, waits for them, and re-layouts  1.32 us (2%)
    pallas_call x1, Pallas kernels, shards(): pl.pallas_call(kernel, out_shape=jax.ShapeDtypeStruct((8 * SLOTS, BS, BS)...  72.7 us

profile of v5, /device:TPU:6, one launch (start us, length us, event | category | flops | bytes accessed | tf_op | source)
XLA Modules:
  0.0 74.1 jit_solution(16281933266947471443)
XLA Ops:
  0.0 72.7 %shard_map.46 = f32[32,128,128]{2,1,0:T(8,128)S(1)} custom-call(f32[512,128]{1,0:T(8,128)} %bitcast.6, f32[512,128]{1,0:T(8,128)} %bitcast.7, s32[4,16]{1,0:T(4,128)} %bitcast.9, s32[7,4,16]{2,1,0:T(4,128)} %bitcast.8), custom_call_target="tpu_custom_call" | custom-call | flops 4000000000 | bytes 5242880 | tf_op jit(solution)/shard_map/pallas_call | solution.py:408
  72.7 1.3 %copy.6 = f32[8,4,128,128]{3,2,1,0:T(8,128)} copy(f32[8,4,128,128]{3,2,1,0:T(8,128)S(1)} %bitcast.5) | data formatting | bytes 4194304

commit v6 on v5

--- a/solution.py
+++ b/solution.py
@@ -14,20 +14,21 @@
 R1 = 208
 GROUP = {1: (0, R1), 2: (R1, DEPTH - R1)}
 ORDER = (
-    ("X", 0), ("P", 1, -1, 0), ("P", 2, 0, -1), ("P", 2, 0, 1), ("X", 1), ("P", 1, 0, -1), ("X", -1), ("N",),
-    ("P", 2, 0, 2), ("X", 2), ("P", 1, 1, 0), ("P", 2, -1, 0), ("P", 2, 0, -2), ("P", 1, 0, 1), ("M", 0), ("M", 1),
-    ("X", -2), ("P", 1, 1, 1), ("P", 2, 1, 0), ("P", 1, -1, 1), ("P", 2, -1, -1), ("P", 1, 0, -2), ("P", 1, 2, 0),
-    ("P", 1, 1, -1), ("P", 2, -1, 1), ("P", 2, 1, -1), ("P", 1, -1, -1), ("P", 1, 0, 2), ("P", 2, 1, 1),
-    ("H", 1, 1, 0), ("H", 1, -1, 0), ("P", 2, 0, 3), ("X", 3), ("H", 1, -1, 1), ("H", 1, 1, 1), ("P", 2, 1, -2),
-    ("C", 0, 1), ("H", 2, 1, 0), ("P", 1, 1, 2), ("H", 2, 1, 1), ("P", 2, 1, 2), ("P", 2, -1, 2), ("H", 2, -1, 0),
-    ("P", 1, 0, 3), ("P", 2, 0, -3), ("X", -3), ("P", 1, -1, 2), ("P", 1, 1, -2), ("P", 1, 2, -1), ("C", 1, 1),
-    ("P", 2, 2, 0), ("H", 3, 1, 0), ("P", 2, 0, 4), ("H", 2, -1, 1), ("P", 1, 2, 1), ("X", 4), ("C", 1, -1),
-    ("P", 1, -1, -2), ("C", 2, 1), ("H", 3, 1, 1), ("P", 2, -1, -2), ("P", 2, 2, 1), ("P", 1, 0, -3), ("P", 2, -1, 3),
-    ("H", 3, -1, 0), ("P", 1, 1, 3), ("C", 2, -1), ("H", 3, -1, 1), ("P", 1, -1, 3), ("P", 1, 1, -3), ("P", 2, 1, -3),
-    ("H", 4, 1, 0), ("P", 2, 2, 2), ("P", 2, 2, -1), ("C", 3, -1), ("P", 2, 2, -2), ("P", 1, 1, 4), ("H", 4, 1, 1),
-    ("C", 3, 1), ("P", 1, 2, 2), ("P", 2, -1, -3), ("P", 1, -1, 4), ("P", 1, 0, 4), ("P", 2, 1, 4), ("P", 2, 1, 3),
-    ("P", 1, -1, -3), ("P", 1, 2, -2), ("C", 4, 1), ("P", 2, -1, 4), ("Q", 0), ("Q", 1), ("P", 1, 2, 3), ("Q", 3),
-    ("P", 1, 2, -3), ("Q", 2), ("P", 2, 2, 4), ("P", 2, 2, -3), ("P", 1, 2, 4), ("P", 2, 2, 3),
+    ("X", 0), ("Z",), ("P", 1, 1, 0), ("P", 2, 0, 1), ("P", 1, -1, 0), ("P", 2, 0, -1), ("X", 1), ("P", 1, 0, -1),
+    ("X", -1), ("P", 1, 0, 1), ("N",), ("P", 2, 0, 2), ("X", 2), ("P", 1, 1, 1), ("P", 2, 0, -2), ("X", -2),
+    ("P", 2, -1, 0), ("M", 0), ("P", 1, 0, -2), ("P", 1, 0, 2), ("P", 2, 1, 0), ("M", 1), ("P", 1, 2, 0),
+    ("P", 1, -1, 1), ("P", 2, -1, 1), ("P", 2, -1, -1), ("P", 2, 1, -1), ("H", 1, 1, 0), ("P", 2, 1, 1),
+    ("P", 1, 1, -1), ("H", 1, -1, 0), ("P", 2, 1, -2), ("H", 1, 1, 1), ("P", 2, 0, 3), ("X", 3), ("P", 1, 0, -3),
+    ("H", 1, -1, 1), ("P", 1, -1, -1), ("P", 1, 1, 2), ("H", 2, 1, 0), ("P", 2, 0, -3), ("C", 0, 1), ("X", -3),
+    ("P", 1, 0, 3), ("H", 2, 1, 1), ("C", 1, 1), ("P", 2, 1, 2), ("H", 3, 1, 0), ("P", 1, -1, 2), ("H", 2, -1, 0),
+    ("P", 1, 1, -2), ("P", 1, 2, -1), ("H", 2, -1, 1), ("P", 2, -1, 2), ("P", 1, -1, -2), ("P", 2, 0, 4), ("X", 4),
+    ("P", 1, 2, 1), ("C", 1, -1), ("C", 2, 1), ("H", 3, 1, 1), ("P", 1, 1, 3), ("P", 2, -1, 3), ("C", 2, -1),
+    ("P", 2, -1, -2), ("H", 4, 1, 0), ("P", 2, 2, 0), ("P", 2, 2, -1), ("P", 1, -1, 3), ("P", 2, 2, 1),
+    ("P", 1, 1, -3), ("P", 2, 2, -2), ("P", 2, 1, -3), ("H", 3, -1, 0), ("P", 1, 2, 2), ("P", 1, 1, 4),
+    ("P", 2, 2, 2), ("H", 4, 1, 1), ("P", 1, 0, 4), ("H", 3, -1, 1), ("C", 3, -1), ("P", 2, 1, 3), ("P", 2, 1, 4),
+    ("C", 4, 1), ("P", 1, -1, -3), ("P", 1, -1, 4), ("P", 1, 2, -2), ("P", 1, 2, 3), ("C", 3, 1), ("P", 2, -1, -3),
+    ("P", 2, 2, -3), ("P", 2, -1, 4), ("Q", 1), ("Q", 0), ("Q", 3), ("P", 2, 2, 4), ("P", 1, 2, -3), ("P", 2, 2, 3),
+    ("Q", 2), ("P", 1, 2, 4),
 )
 QUARTERS = 4
 
@@ -63,7 +64,7 @@
     a_ref, p_ref, cols_ref, codes_ref, out_ref,
     p_own, p_opp, ps_own, ps_opp, a_all, sums, cols, codes_in, codes_own, codes_opp,
     picks_own, picks_opp, picks_smem_own, picks_smem_opp,
-    passing, p_recv, p_send, a_recv, a_send, sib_recv, sib_send, move_send, pass_sem, codes_sem, local_sem,
+    passing, p_recv, p_send, a_recv, a_send, sib_recv, sib_send, move_send, pass_sem, codes_sem, local_sem, plane_ready, line_ready,
 ):
     row, col, layer = lax.axis_index("row"), lax.axis_index("col"), lax.axis_index("layer")
     y, z, core = lax.rem(row, NY), col // 2, lax.rem(col, 2)
@@ -93,10 +94,22 @@
     cols_load.start()
 
     barrier = pltpu.get_barrier_semaphore()
-    greeted = [along(axis, way) for axis in "xyz" for way in (1, -1)] + [sibling, mover, opposite]
-    for other in greeted:
-        pl.semaphore_signal(barrier, inc=1, device_id=other, device_id_type=MESH)
-    pl.semaphore_wait(barrier, len(greeted))
+    for axis in "xy":
+        for way in (1, -1):
+            row_, _, layer_ = along(axis, way)
+            pl.semaphore_signal(barrier, inc=1, device_id=(row_, z * 2, layer_), device_id_type=MESH)
+    for row_, col_, layer_ in (along("z", 1), along("z", -1), mover, opposite):
+        pl.semaphore_signal(barrier, inc=1, device_id=(row_, (col_ // 2) * 2 + 1, layer_), device_id_type=MESH)
+
+    @pl.when(core == 0)
+    def _():
+        pl.semaphore_wait(barrier, 9)
+        pl.semaphore_signal(plane_ready, inc=1, device_id=sibling, device_id_type=MESH)
+
+    @pl.when(core == 1)
+    def _():
+        pl.semaphore_signal(barrier, inc=1, device_id=sibling, device_id_type=MESH)
+        pl.semaphore_wait(plane_ready, 1)
 
     p_land = (p_own, p_opp)
     p_split = (ps_own, ps_opp)
@@ -284,21 +297,16 @@
     p_local = pltpu.make_async_copy(p_ref, p_own.at[q_me], local_sem.at[0])
     a_local = pltpu.make_async_copy(a_ref, a_all.at[rows_of(lax.rem(t, 4)) + core], local_sem.at[1])
 
-    @pl.when(t >= 4)
-    def _():
-        move_copy.start()
-        pass_copy.start()
-
-    for copy in p_forward(1, 0, 0) + p_forward(2, 0, 0, "y"):
-        copy.start()
-
-    @pl.when(t < 4)
-    def _():
-        for h in range(2):
-            for way in (1, -1):
-                a_copy(t, h, 0, way, a_ref.at[pl.ds(h * half, half)]).start()
-        a_local.start()
-        sib_copy(t, a_ref).start()
+    begun = []
+    left = []
+    now = -1
+
+    def start(*copies):
+        for copy in copies:
+            copy.start()
+            left.append((now, copy.wait_send))
+
+    start(*p_forward(2, 0, 0, "y"), *p_forward(1, 0, 0))
 
     p_local.start()
     codes_own[...] = jnp.full(codes_own.shape, SLOTS * SLOTS, jnp.int32)
@@ -310,20 +318,19 @@
     sums[:, 0] = jnp.zeros((16, 2 * BS, BS), jnp.bfloat16)
     p_local.wait()
     p_convert(0, 0, 0, DEPTH)
-    codes_copy.wait()
-    pick(1)
-    for which in range(2):
-        pick_copy(which).wait()
+    pick_copy(0).wait()
+
+    def other_codes():
+        codes_copy.wait()
+        pick(1)
 
     def piece_of_p(g, a, b):
         p_wait(g, a, b)
-        for copy in p_forward(g, a, b, "y" if (g, a) == (2, 0) else "xy"):
-            copy.start()
+        start(*p_forward(g, a, b, "y" if (g, a) == (2, 0) else "xy"))
         p_convert(a, b, *GROUP[g])
 
     def across(b):
-        for copy in p_forward(2, 0, b, "x"):
-            copy.start()
+        start(*p_forward(2, 0, b, "x"))
 
     def moved(h):
         @pl.when(t >= 4)
@@ -334,6 +341,34 @@
             if h == 1:
                 sib_copy(t).start()
 
+        for way in (1, -1):
+            left.append((now, a_copy(t, h, 0, way).wait_send))
+        if h == 1:
+            left.append((now, sib_copy(t).wait_send))
+
+    def line():
+        @pl.when(core == 1)
+        def _():
+            pl.semaphore_wait(barrier, 8)
+            pl.semaphore_signal(line_ready, inc=1, device_id=sibling, device_id_type=MESH)
+
+        @pl.when(core == 0)
+        def _():
+            pl.semaphore_wait(line_ready, 1)
+
+        @pl.when(t >= 4)
+        def _():
+            move_copy.start()
+            pass_copy.start()
+
+        @pl.when(t < 4)
+        def _():
+            for h in range(2):
+                for way in (1, -1):
+                    a_copy(t, h, 0, way, a_ref.at[pl.ds(h * half, half)]).start()
+            a_local.start()
+            sib_copy(t, a_ref).start()
+
     def cross():
         @pl.when(t < 4)
         def _():
@@ -344,9 +379,9 @@
         e = source(d, way)
         a_wait(e, h)
         if goes_on(d, way):
-            a_copy(e, h, d, way).start()
+            start(a_copy(e, h, d, way))
         if h == 1:
-            sib_copy(e).start()
+            start(sib_copy(e))
 
     def add_up(d, way):
         if d == 0:
@@ -360,18 +395,25 @@
         combine(e)
 
     def quarter(i):
+        if not begun:
+            pick_copy(1).wait()
+            begun.append(i)
         products(1, i * 8 // QUARTERS, 8 // QUARTERS)
 
-    steps = {"P": piece_of_p, "M": moved, "H": hop, "C": add_up, "N": cross, "X": across, "Q": quarter}
-    for name, *where in ORDER:
+    steps = {"P": piece_of_p, "M": moved, "H": hop, "C": add_up, "N": cross, "Z": line, "X": across, "Q": quarter}
+    for now, (name, *where) in enumerate(ORDER):
+        if now == 20:
+            other_codes()
+        if now == len(ORDER) - 3:
+            for began, wait in left:
+                if began < now - 20:
+                    wait()
+            left = [entry for entry in left if entry[0] >= now - 20]
         steps[name](*where)
     products(0, 0, 8)
 
-    for g in (1, 2):
-        for a in range(-1, 3):
-            for b in range(-3, 5):
-                for copy in p_forward(g, a, b):
-                    copy.wait_send()
+    for _, wait in left:
+        wait()
 
     @pl.when(t >= 4)
     def _():
@@ -381,18 +423,6 @@
     @pl.when(t < 4)
     def _():
         cross_copy.wait_send()
-
-    for d in range(5):
-        for way in (1, -1):
-            if (d == 4 and way == -1) or (d == 0 and way == -1):
-                continue
-            e = source(d, way)
-            sib_copy(e).wait_send()
-    for d in range(4):
-        for way in (1, -1):
-            if goes_on(d, way):
-                for h in range(2):
-                    a_copy(source(d, way), h, d, way).wait_send()
 
 
 def shards(a_blocks, p_blocks, out_columns, pair_codes):
@@ -441,6 +471,8 @@
             dma((2,)),
             dma((2,)),
             dma((6,)),
+            pltpu.SemaphoreType.REGULAR,
+            pltpu.SemaphoreType.REGULAR,
         ],
         compiler_params=pltpu.CompilerParams(
             collective_id=0, has_side_effects=True, vmem_limit_bytes=44 * 2**20

time: 74.2 us -> 70.3 us (0.947)
  Pallas kernels: 72.7 us -> 68.2 us
    pallas_call x1, Pallas kernels: 72.7 us -> 68.2 us  [shards(): pl.pallas_call(kernel, out_shape=jax.ShapeDtypeStruct((8 * SLOTS, BS, BS)...]
where the time goes in v6:
time: 70.3 us; the launch traced here: 69.5 us
  Pallas kernels  68.2 us (97%)
  local copies, waits for them, and re-layouts  1.32 us (2%)
    pallas_call x1, Pallas kernels, shards(): pl.pallas_call(kernel, out_shape=jax.ShapeDtypeStruct((8 * SLOTS, BS, BS)...  68.2 us

profile of v6, /device:TPU:6, one launch (start us, length us, event | category | flops | bytes accessed | tf_op | source)
XLA Modules:
  0.0 69.5 jit_solution(12694368582442023909)
XLA Ops:
  0.0 68.2 %shard_map.46 = f32[32,128,128]{2,1,0:T(8,128)S(1)} custom-call(f32[512,128]{1,0:T(8,128)} %bitcast.6, f32[512,128]{1,0:T(8,128)} %bitcast.7, s32[4,16]{1,0:T(4,128)} %bitcast.9, s32[7,4,16]{2,1,0:T(4,128)} %bitcast.8), custom_call_target="tpu_custom_call" | custom-call | flops 4000000000 | bytes 5242880 | tf_op jit(solution)/shard_map/pallas_call | solution.py:438
  68.2 1.3 %copy.6 = f32[8,4,128,128]{3,2,1,0:T(8,128)} copy(f32[8,4,128,128]{3,2,1,0:T(8,128)S(1)} %bitcast.5) | data formatting | bytes 4194304

commit v7 on v6

--- a/solution.py
+++ b/solution.py
@@ -14,21 +14,21 @@
 R1 = 208
 GROUP = {1: (0, R1), 2: (R1, DEPTH - R1)}
 ORDER = (
-    ("X", 0), ("Z",), ("P", 1, 1, 0), ("P", 2, 0, 1), ("P", 1, -1, 0), ("P", 2, 0, -1), ("X", 1), ("P", 1, 0, -1),
-    ("X", -1), ("P", 1, 0, 1), ("N",), ("P", 2, 0, 2), ("X", 2), ("P", 1, 1, 1), ("P", 2, 0, -2), ("X", -2),
-    ("P", 2, -1, 0), ("M", 0), ("P", 1, 0, -2), ("P", 1, 0, 2), ("P", 2, 1, 0), ("M", 1), ("P", 1, 2, 0),
-    ("P", 1, -1, 1), ("P", 2, -1, 1), ("P", 2, -1, -1), ("P", 2, 1, -1), ("H", 1, 1, 0), ("P", 2, 1, 1),
-    ("P", 1, 1, -1), ("H", 1, -1, 0), ("P", 2, 1, -2), ("H", 1, 1, 1), ("P", 2, 0, 3), ("X", 3), ("P", 1, 0, -3),
-    ("H", 1, -1, 1), ("P", 1, -1, -1), ("P", 1, 1, 2), ("H", 2, 1, 0), ("P", 2, 0, -3), ("C", 0, 1), ("X", -3),
-    ("P", 1, 0, 3), ("H", 2, 1, 1), ("C", 1, 1), ("P", 2, 1, 2), ("H", 3, 1, 0), ("P", 1, -1, 2), ("H", 2, -1, 0),
-    ("P", 1, 1, -2), ("P", 1, 2, -1), ("H", 2, -1, 1), ("P", 2, -1, 2), ("P", 1, -1, -2), ("P", 2, 0, 4), ("X", 4),
-    ("P", 1, 2, 1), ("C", 1, -1), ("C", 2, 1), ("H", 3, 1, 1), ("P", 1, 1, 3), ("P", 2, -1, 3), ("C", 2, -1),
-    ("P", 2, -1, -2), ("H", 4, 1, 0), ("P", 2, 2, 0), ("P", 2, 2, -1), ("P", 1, -1, 3), ("P", 2, 2, 1),
-    ("P", 1, 1, -3), ("P", 2, 2, -2), ("P", 2, 1, -3), ("H", 3, -1, 0), ("P", 1, 2, 2), ("P", 1, 1, 4),
-    ("P", 2, 2, 2), ("H", 4, 1, 1), ("P", 1, 0, 4), ("H", 3, -1, 1), ("C", 3, -1), ("P", 2, 1, 3), ("P", 2, 1, 4),
-    ("C", 4, 1), ("P", 1, -1, -3), ("P", 1, -1, 4), ("P", 1, 2, -2), ("P", 1, 2, 3), ("C", 3, 1), ("P", 2, -1, -3),
-    ("P", 2, 2, -3), ("P", 2, -1, 4), ("Q", 1), ("Q", 0), ("Q", 3), ("P", 2, 2, 4), ("P", 1, 2, -3), ("P", 2, 2, 3),
-    ("Q", 2), ("P", 1, 2, 4),
+    ("X", 0), ("Z",), ("P", 1, 1, 0), ("P", 2, 0, 1), ("X", 1), ("P", 1, 0, -1), ("P", 2, 0, -1), ("X", -1),
+    ("P", 1, -1, 0), ("N",), ("P", 1, 0, 1), ("P", 2, 0, 2), ("X", 2), ("P", 2, 0, -2), ("X", -2), ("P", 1, 1, 1),
+    ("M", 0), ("P", 1, 0, -2), ("P", 2, -1, 0), ("P", 1, 2, 0), ("P", 2, -1, 1), ("P", 1, 0, 2), ("M", 1),
+    ("P", 2, 1, 0), ("P", 1, -1, 1), ("P", 2, 1, -1), ("H", 1, -1, 0), ("P", 1, 1, -1), ("P", 2, 1, -2),
+    ("H", 1, 1, 0), ("P", 2, 1, 1), ("P", 1, 1, 2), ("H", 1, 1, 1), ("P", 2, -1, -1), ("P", 2, 0, 3), ("X", 3),
+    ("P", 1, 0, -3), ("P", 2, 0, -3), ("X", -3), ("H", 2, 1, 0), ("P", 1, -1, -1), ("H", 1, -1, 1), ("P", 1, 2, -1),
+    ("C", 0, 1), ("H", 2, 1, 1), ("C", 1, 1), ("P", 1, 1, -2), ("H", 3, 1, 0), ("P", 1, 2, 1), ("P", 1, 0, 3),
+    ("P", 1, -1, 2), ("H", 2, -1, 0), ("P", 2, -1, 2), ("H", 2, -1, 1), ("P", 2, 2, 1), ("H", 3, 1, 1),
+    ("P", 2, 0, 4), ("X", 4), ("P", 1, 1, 3), ("C", 1, -1), ("C", 2, 1), ("P", 1, -1, -2), ("C", 2, -1),
+    ("P", 2, -1, 3), ("P", 2, -1, -2), ("P", 2, 1, 2), ("H", 4, 1, 0), ("P", 2, 2, -1), ("P", 1, 2, 2),
+    ("P", 1, -1, 3), ("P", 1, 1, -3), ("H", 3, -1, 0), ("P", 2, 2, -2), ("P", 2, 1, -3), ("P", 1, 2, -2),
+    ("H", 3, -1, 1), ("C", 3, -1), ("H", 4, 1, 1), ("P", 1, -1, -3), ("P", 2, 1, 3), ("P", 2, 1, 4), ("P", 1, 1, 4),
+    ("C", 3, 1), ("P", 2, -1, -3), ("P", 2, 2, 0), ("P", 1, 2, 3), ("P", 2, -1, 4), ("P", 2, 2, 2), ("P", 1, -1, 4),
+    ("C", 4, 1), ("Q", 0), ("P", 1, 2, -3), ("P", 1, 0, 4), ("P", 1, 2, 4), ("Q", 2), ("Q", 1), ("Q", 3),
+    ("P", 2, 2, 4), ("P", 2, 2, -3), ("P", 2, 2, 3),
 )
 QUARTERS = 4
 
@@ -281,18 +281,19 @@
 
     def products(which, first, count):
         def step(i, carry):
-            r = first + i
-            at = 8 * layer + r
-            for o in range(SLOTS):
-                q = cols[o, at]
-                left = jnp.concatenate([sums[8 * which + r, picks_smem[which][p, o, at]] for p in range(SLOTS)], axis=1)
-                four = jnp.dot(left, p_split[which][q], preferred_element_type=jnp.float32)
-                value = (four[BS:, BS:] + four[:BS, BS:] + four[BS:, :BS]) + four[:BS, :BS]
-                where = r * SLOTS + o
-                out_ref[where] = value if which == 1 else out_ref[where] + value
+            for j in range(2):
+                r = first + 2 * i + j
+                at = 8 * layer + r
+                for o in range(SLOTS):
+                    q = cols[o, at]
+                    left = jnp.concatenate([sums[8 * which + r, picks_smem[which][p, o, at]] for p in range(SLOTS)], axis=1)
+                    four = jnp.dot(left, p_split[which][q], preferred_element_type=jnp.float32)
+                    value = (four[BS:, BS:] + four[:BS, BS:] + four[BS:, :BS]) + four[:BS, :BS]
+                    where = r * SLOTS + o
+                    out_ref[where] = value if which == 1 else out_ref[where] + value
             return carry
 
-        lax.fori_loop(0, count, step, 0)
+        lax.fori_loop(0, count // 2, step, 0)
 
     p_local = pltpu.make_async_copy(p_ref, p_own.at[q_me], local_sem.at[0])
     a_local = pltpu.make_async_copy(a_ref, a_all.at[rows_of(lax.rem(t, 4)) + core], local_sem.at[1])

time: 70.3 us -> 70.3 us (level)
  the two profiles are of different devices: /device:TPU:6 before, /device:TPU:66 now
where the time goes in v7:
time: 70.3 us; the launch traced here: 70.2 us
  Pallas kernels  68.8 us (98%)
  local copies, waits for them, and re-layouts  1.32 us (2%)
    pallas_call x1, Pallas kernels, shards(): pl.pallas_call(kernel, out_shape=jax.ShapeDtypeStruct((8 * SLOTS, BS, BS)...  68.8 us

profile of v7, /device:TPU:66, one launch (start us, length us, event | category | flops | bytes accessed | tf_op | source)
XLA Modules:
  0.0 70.2 jit_solution(8745777078268744732)
XLA Ops:
  0.0 68.8 %shard_map.46 = f32[32,128,128]{2,1,0:T(8,128)S(1)} custom-call(f32[512,128]{1,0:T(8,128)} %bitcast.6, f32[512,128]{1,0:T(8,128)} %bitcast.7, s32[4,16]{1,0:T(4,128)} %bitcast.9, s32[7,4,16]{2,1,0:T(4,128)} %bitcast.8), custom_call_target="tpu_custom_call" | custom-call | flops 4000000000 | bytes 5242880 | tf_op jit(solution)/shard_map/pallas_call | solution.py:439
  68.9 1.3 %copy.6 = f32[8,4,128,128]{3,2,1,0:T(8,128)} copy(f32[8,4,128,128]{3,2,1,0:T(8,128)S(1)} %bitcast.5) | data formatting | bytes 4194304

commit v8 on v6

--- a/solution.py
+++ b/solution.py
@@ -14,23 +14,22 @@
 R1 = 208
 GROUP = {1: (0, R1), 2: (R1, DEPTH - R1)}
 ORDER = (
-    ("X", 0), ("Z",), ("P", 1, 1, 0), ("P", 2, 0, 1), ("P", 1, -1, 0), ("P", 2, 0, -1), ("X", 1), ("P", 1, 0, -1),
-    ("X", -1), ("P", 1, 0, 1), ("N",), ("P", 2, 0, 2), ("X", 2), ("P", 1, 1, 1), ("P", 2, 0, -2), ("X", -2),
-    ("P", 2, -1, 0), ("M", 0), ("P", 1, 0, -2), ("P", 1, 0, 2), ("P", 2, 1, 0), ("M", 1), ("P", 1, 2, 0),
-    ("P", 1, -1, 1), ("P", 2, -1, 1), ("P", 2, -1, -1), ("P", 2, 1, -1), ("H", 1, 1, 0), ("P", 2, 1, 1),
-    ("P", 1, 1, -1), ("H", 1, -1, 0), ("P", 2, 1, -2), ("H", 1, 1, 1), ("P", 2, 0, 3), ("X", 3), ("P", 1, 0, -3),
-    ("H", 1, -1, 1), ("P", 1, -1, -1), ("P", 1, 1, 2), ("H", 2, 1, 0), ("P", 2, 0, -3), ("C", 0, 1), ("X", -3),
-    ("P", 1, 0, 3), ("H", 2, 1, 1), ("C", 1, 1), ("P", 2, 1, 2), ("H", 3, 1, 0), ("P", 1, -1, 2), ("H", 2, -1, 0),
-    ("P", 1, 1, -2), ("P", 1, 2, -1), ("H", 2, -1, 1), ("P", 2, -1, 2), ("P", 1, -1, -2), ("P", 2, 0, 4), ("X", 4),
-    ("P", 1, 2, 1), ("C", 1, -1), ("C", 2, 1), ("H", 3, 1, 1), ("P", 1, 1, 3), ("P", 2, -1, 3), ("C", 2, -1),
-    ("P", 2, -1, -2), ("H", 4, 1, 0), ("P", 2, 2, 0), ("P", 2, 2, -1), ("P", 1, -1, 3), ("P", 2, 2, 1),
-    ("P", 1, 1, -3), ("P", 2, 2, -2), ("P", 2, 1, -3), ("H", 3, -1, 0), ("P", 1, 2, 2), ("P", 1, 1, 4),
-    ("P", 2, 2, 2), ("H", 4, 1, 1), ("P", 1, 0, 4), ("H", 3, -1, 1), ("C", 3, -1), ("P", 2, 1, 3), ("P", 2, 1, 4),
-    ("C", 4, 1), ("P", 1, -1, -3), ("P", 1, -1, 4), ("P", 1, 2, -2), ("P", 1, 2, 3), ("C", 3, 1), ("P", 2, -1, -3),
-    ("P", 2, 2, -3), ("P", 2, -1, 4), ("Q", 1), ("Q", 0), ("Q", 3), ("P", 2, 2, 4), ("P", 1, 2, -3), ("P", 2, 2, 3),
-    ("Q", 2), ("P", 1, 2, 4),
+    ("X", 0), ("Z",), ("P", 1, 1, 0), ("P", 2, 0, 1), ("X", 1), ("P", 1, 0, -1), ("P", 2, 0, -1), ("X", -1),
+    ("P", 1, -1, 0), ("N",), ("P", 1, 0, 1), ("P", 2, 0, 2), ("X", 2), ("P", 2, 0, -2), ("X", -2), ("P", 1, 1, 1),
+    ("P", 1, 0, -2), ("P", 1, 2, 0), ("P", 2, -1, 0), ("M", 0), ("P", 1, 0, 2), ("P", 2, -1, 1), ("P", 2, 1, 1),
+    ("P", 2, 1, 0), ("P", 1, -1, 1), ("P", 2, 1, -1), ("M", 1), ("H", 1, -1, 0), ("P", 1, 1, -1), ("H", 1, 1, 0),
+    ("P", 2, 1, -2), ("H", 1, 1, 1), ("P", 1, 1, 2), ("P", 2, -1, -1), ("P", 2, 0, 3), ("X", 3), ("P", 1, 0, -3),
+    ("P", 2, 0, -3), ("X", -3), ("H", 2, 1, 0), ("P", 1, -1, -1), ("H", 1, -1, 1), ("P", 1, 2, -1), ("C", 0, 1),
+    ("H", 2, 1, 1), ("P", 1, 1, -2), ("C", 1, 1), ("H", 3, 1, 0), ("P", 2, -1, 2), ("P", 1, 2, 1), ("H", 2, -1, 0),
+    ("P", 1, 0, 3), ("P", 1, -1, 2), ("H", 2, -1, 1), ("H", 3, 1, 1), ("P", 2, 0, 4), ("P", 2, 2, 1), ("X", 4),
+    ("P", 1, 1, 3), ("C", 1, -1), ("C", 2, 1), ("P", 1, -1, -2), ("C", 2, -1), ("P", 2, 1, 2), ("P", 2, -1, 3),
+    ("P", 2, -1, -2), ("H", 4, 1, 0), ("P", 2, 2, -1), ("P", 1, 2, 2), ("P", 1, -1, 3), ("P", 1, 1, -3),
+    ("P", 1, 1, 4), ("H", 3, -1, 0), ("P", 2, 2, -2), ("P", 2, 1, -3), ("P", 1, 2, -2), ("H", 3, -1, 1),
+    ("H", 4, 1, 1), ("C", 3, -1), ("P", 1, -1, -3), ("P", 2, 1, 3), ("P", 2, 1, 4), ("C", 3, 1), ("P", 1, 2, 3),
+    ("P", 2, 2, 0), ("P", 2, -1, -3), ("P", 1, -1, 4), ("P", 2, -1, 4), ("O", 1, 1), ("P", 2, 2, 2), ("C", 4, 1),
+    ("P", 1, 2, -3), ("O", 1, -1), ("O", 0, 1), ("O", 2, 1), ("O", 2, -1), ("O", 3, 1), ("O", 3, -1), ("O", 4, 1),
+    ("P", 1, 0, 4), ("P", 2, 2, 4), ("P", 1, 2, 4), ("P", 2, 2, -3), ("P", 2, 2, 3),
 )
-QUARTERS = 4
 
 
 def onward(g, a, b):
@@ -394,13 +393,17 @@
         sib_wait(e)
         combine(e)
 
-    def quarter(i):
+    def piece_products(d, way):
         if not begun:
             pick_copy(1).wait()
-            begun.append(i)
-        products(1, i * 8 // QUARTERS, 8 // QUARTERS)
-
-    steps = {"P": piece_of_p, "M": moved, "H": hop, "C": add_up, "N": cross, "Z": line, "X": across, "Q": quarter}
+            begun.append(d)
+        e = source(d, way)
+
+        @pl.when(e >= 4)
+        def _():
+            products(1, rows_of(e) - 8, 2)
+
+    steps = {"P": piece_of_p, "M": moved, "H": hop, "C": add_up, "N": cross, "Z": line, "X": across, "O": piece_products}
     for now, (name, *where) in enumerate(ORDER):
         if now == 20:
             other_codes()

time: 70.3 us -> 69.9 us (level)
  Pallas kernels: 68.2 us -> 67.3 us
    pallas_call x1, Pallas kernels: 68.2 us -> 67.3 us  [shards(): pl.pallas_call(kernel, out_shape=jax.ShapeDtypeStruct((8 * SLOTS, BS, BS)...]
where the time goes in v8:
time: 69.9 us; the launch traced here: 68.7 us
  Pallas kernels  67.3 us (96%)
  local copies, waits for them, and re-layouts  1.32 us (2%)
    pallas_call x1, Pallas kernels, shards(): pl.pallas_call(kernel, out_shape=jax.ShapeDtypeStruct((8 * SLOTS, BS, BS)...  67.3 us

profile of v8, /device:TPU:6, one launch (start us, length us, event | category | flops | bytes accessed | tf_op | source)
XLA Modules:
  0.0 68.7 jit_solution(13485711467200424961)
XLA Ops:
  0.0 67.3 %shard_map.46 = f32[32,128,128]{2,1,0:T(8,128)S(1)} custom-call(f32[512,128]{1,0:T(8,128)} %bitcast.6, f32[512,128]{1,0:T(8,128)} %bitcast.7, s32[4,16]{1,0:T(4,128)} %bitcast.9, s32[7,4,16]{2,1,0:T(4,128)} %bitcast.8), custom_call_target="tpu_custom_call" | custom-call | flops 4000000000 | bytes 5242880 | tf_op jit(solution)/shard_map/pallas_call | solution.py:441
  67.3 1.3 %copy.6 = f32[8,4,128,128]{3,2,1,0:T(8,128)} copy(f32[8,4,128,128]{3,2,1,0:T(8,128)S(1)} %bitcast.5) | data formatting | bytes 4194304

commit v9 on v8

--- a/solution.py
+++ b/solution.py
@@ -16,19 +16,19 @@
 ORDER = (
     ("X", 0), ("Z",), ("P", 1, 1, 0), ("P", 2, 0, 1), ("X", 1), ("P", 1, 0, -1), ("P", 2, 0, -1), ("X", -1),
     ("P", 1, -1, 0), ("N",), ("P", 1, 0, 1), ("P", 2, 0, 2), ("X", 2), ("P", 2, 0, -2), ("X", -2), ("P", 1, 1, 1),
-    ("P", 1, 0, -2), ("P", 1, 2, 0), ("P", 2, -1, 0), ("M", 0), ("P", 1, 0, 2), ("P", 2, -1, 1), ("P", 2, 1, 1),
-    ("P", 2, 1, 0), ("P", 1, -1, 1), ("P", 2, 1, -1), ("M", 1), ("H", 1, -1, 0), ("P", 1, 1, -1), ("H", 1, 1, 0),
-    ("P", 2, 1, -2), ("H", 1, 1, 1), ("P", 1, 1, 2), ("P", 2, -1, -1), ("P", 2, 0, 3), ("X", 3), ("P", 1, 0, -3),
-    ("P", 2, 0, -3), ("X", -3), ("H", 2, 1, 0), ("P", 1, -1, -1), ("H", 1, -1, 1), ("P", 1, 2, -1), ("C", 0, 1),
-    ("H", 2, 1, 1), ("P", 1, 1, -2), ("C", 1, 1), ("H", 3, 1, 0), ("P", 2, -1, 2), ("P", 1, 2, 1), ("H", 2, -1, 0),
-    ("P", 1, 0, 3), ("P", 1, -1, 2), ("H", 2, -1, 1), ("H", 3, 1, 1), ("P", 2, 0, 4), ("P", 2, 2, 1), ("X", 4),
-    ("P", 1, 1, 3), ("C", 1, -1), ("C", 2, 1), ("P", 1, -1, -2), ("C", 2, -1), ("P", 2, 1, 2), ("P", 2, -1, 3),
-    ("P", 2, -1, -2), ("H", 4, 1, 0), ("P", 2, 2, -1), ("P", 1, 2, 2), ("P", 1, -1, 3), ("P", 1, 1, -3),
-    ("P", 1, 1, 4), ("H", 3, -1, 0), ("P", 2, 2, -2), ("P", 2, 1, -3), ("P", 1, 2, -2), ("H", 3, -1, 1),
-    ("H", 4, 1, 1), ("C", 3, -1), ("P", 1, -1, -3), ("P", 2, 1, 3), ("P", 2, 1, 4), ("C", 3, 1), ("P", 1, 2, 3),
-    ("P", 2, 2, 0), ("P", 2, -1, -3), ("P", 1, -1, 4), ("P", 2, -1, 4), ("O", 1, 1), ("P", 2, 2, 2), ("C", 4, 1),
-    ("P", 1, 2, -3), ("O", 1, -1), ("O", 0, 1), ("O", 2, 1), ("O", 2, -1), ("O", 3, 1), ("O", 3, -1), ("O", 4, 1),
-    ("P", 1, 0, 4), ("P", 2, 2, 4), ("P", 1, 2, 4), ("P", 2, 2, -3), ("P", 2, 2, 3),
+    ("P", 1, 0, -2), ("P", 1, 2, 0), ("M", 0), ("P", 2, -1, 0), ("P", 2, -1, 1), ("P", 2, 1, 1), ("P", 1, -1, 1),
+    ("P", 2, 1, 0), ("M", 1), ("P", 1, 0, 2), ("H", 1, -1, 0), ("P", 1, 1, -1), ("H", 1, 1, 0), ("P", 2, 1, -2),
+    ("H", 1, 1, 1), ("P", 2, -1, -1), ("P", 1, 1, 2), ("P", 2, 1, -1), ("P", 2, 0, 3), ("X", 3), ("P", 1, 0, -3),
+    ("P", 2, 0, -3), ("X", -3), ("H", 2, 1, 0), ("P", 1, -1, -1), ("H", 1, -1, 1), ("P", 1, 2, -1), ("H", 2, 1, 1),
+    ("P", 1, 1, -2), ("C", 1, 1), ("H", 3, 1, 0), ("P", 1, 2, 1), ("C", 0, 1), ("H", 2, -1, 0), ("P", 1, 0, 3),
+    ("P", 2, -1, 2), ("P", 1, -1, 2), ("H", 2, -1, 1), ("C", 1, -1), ("H", 3, 1, 1), ("C", 2, 1), ("P", 1, 1, 3),
+    ("P", 2, 0, 4), ("X", 4), ("C", 2, -1), ("P", 2, 2, 1), ("P", 2, 2, -1), ("P", 1, -1, -2), ("H", 4, 1, 0),
+    ("P", 2, 1, 2), ("P", 2, -1, -2), ("P", 1, 2, 2), ("P", 2, -1, 3), ("P", 1, -1, 3), ("P", 1, 1, -3),
+    ("P", 2, 2, 0), ("P", 2, 1, -3), ("P", 1, 1, 4), ("P", 2, 2, -2), ("H", 3, -1, 0), ("H", 4, 1, 1),
+    ("P", 1, 2, -2), ("H", 3, -1, 1), ("C", 3, -1), ("P", 1, -1, -3), ("P", 2, 1, 4), ("P", 2, 1, 3), ("C", 3, 1),
+    ("P", 1, 2, 3), ("C", 4, 1), ("P", 2, -1, -3), ("P", 2, 2, 2), ("P", 1, -1, 4), ("P", 2, -1, 4), ("O", 1, -1),
+    ("O", 3, -1), ("O", 1, 1), ("O", 2, 1), ("O", 2, -1), ("O", 0, 1), ("O", 3, 1), ("P", 1, 2, -3), ("O", 4, 1),
+    ("P", 2, 2, 3), ("P", 2, 2, 4), ("P", 1, 0, 4), ("P", 2, 2, -3), ("P", 1, 2, 4),
 )
 
 

time: 69.9 us -> 69.7 us (level)
  no operation moved by 1% of the time
where the time goes in v9:
time: 69.7 us; the launch traced here: 68.7 us
  Pallas kernels  67.4 us (97%)
  local copies, waits for them, and re-layouts  1.32 us (2%)
    pallas_call x1, Pallas kernels, shards(): pl.pallas_call(kernel, out_shape=jax.ShapeDtypeStruct((8 * SLOTS, BS, BS)...  67.4 us

profile of v9, /device:TPU:6, one launch (start us, length us, event | category | flops | bytes accessed | tf_op | source)
XLA Modules:
  0.0 68.7 jit_solution(8221275078255967741)
XLA Ops:
  0.0 67.4 %shard_map.46 = f32[32,128,128]{2,1,0:T(8,128)S(1)} custom-call(f32[512,128]{1,0:T(8,128)} %bitcast.6, f32[512,128]{1,0:T(8,128)} %bitcast.7, s32[4,16]{1,0:T(4,128)} %bitcast.9, s32[7,4,16]{2,1,0:T(4,128)} %bitcast.8), custom_call_target="tpu_custom_call" | custom-call | flops 4000000000 | bytes 5242880 | tf_op jit(solution)/shard_map/pallas_call | solution.py:441
  67.4 1.3 %copy.6 = f32[8,4,128,128]{3,2,1,0:T(8,128)} copy(f32[8,4,128,128]{3,2,1,0:T(8,128)S(1)} %bitcast.5) | data formatting | bytes 4194304
